TPU v7x, 128 devices: a whole 4x4x4 slice. The times are simulated.
128 devices in a mesh: dom: 16 (over z, y_lo, core), loop: 8 (over y_hi, x).
Axes of the slice: x: 4, y: 4 (y_hi: 2, y_lo: 2; y = y_hi * 2 + y_lo), z: 4, core: 2. Of those that a mesh axis runs over, the one named last changes fastest.
Arguments:
- cotangent: bfloat16 [131072, 256], P(('dom', 'loop')), may hold values from -6 to 6
- preact: bfloat16 [131072, 256], P(('dom', 'loop')), may hold values from -6 to 6
- aggregated: bfloat16 [131072, 256], P(('dom', 'loop')), may hold values from -6 to 6
- weight: bfloat16 [256, 256], replicated, may hold values from -0.375 to 0.375
- tile_values: bfloat16 [81920, 128, 128], P(('dom', 'loop')), as said below
- tile_rows: int32 [128, 640], P(('dom', 'loop')), may hold values from 0 to 63
- tile_cols: int32 [128, 640], P(('dom', 'loop')), may hold values from 0 to 127, as said below
- tile_counts: int32 [128], P(('dom', 'loop')), may hold values from 64 to 640
Outputs:
- node_grad: float32 [131072, 256], P(('dom', 'loop'))
- weight_grad: float32 [256, 256], replicated
Inputs may be any that keep to these rules, and one draw needn't show every extreme that they name: `tile_cols`: the live tiles of one device touch, for every dom index, exactly 4 distinct column blocks, and every tile's column lies among them. `tile_values`: entries are nonnegative.
All inputs are finite; a program needn't handle non-finite values.
Results may differ from a plain program's by a relative error of at most 0.0029.
Values may be sent and summed in bfloat16 or wider, within the bound.
A program may use at most 192 MiB of HBM per device.

v0:
```python
import math

import jax
import jax.numpy as jnp
from jax import lax
from jax.sharding import PartitionSpec as P


def shards(cotangent, preact, aggregated, weight, tile_values, tile_rows, tile_cols, tile_counts):
    node_rows, width = cotangent.shape
    tile_size = tile_values.shape[1]
    dom_count = lax.axis_size("dom")
    total_nodes = node_rows * dom_count * lax.axis_size("loop")
    local_blocks = node_rows // tile_size
    all_blocks = dom_count * local_blocks
    masked = jnp.where(preact > 0, cotangent, jnp.zeros_like(cotangent))
    weight_term = jnp.dot(aggregated.T, masked, preferred_element_type=jnp.float32) * (
        1.0 / math.sqrt(total_nodes)
    )
    weight_grad = lax.psum(weight_term, ("dom", "loop"))
    projected = jnp.dot(masked, weight.T, preferred_element_type=jnp.float32).astype(jnp.bfloat16)
    partition = lax.all_gather(projected, "loop", axis=0, tiled=True)
    part_blocks = partition.shape[0] // tile_size
    flat_rows = partition.reshape(part_blocks, tile_size * width)
    tile_total = tile_rows.shape[1]
    live = (jnp.arange(tile_total, dtype=jnp.int32) < tile_counts[0]).astype(jnp.float32)
    group_size = math.gcd(tile_total, 64)
    groups = tile_total // group_size
    row_ids = jnp.arange(part_blocks, dtype=jnp.int32)
    col_ids = jnp.arange(all_blocks, dtype=jnp.int32)

    def accumulate(totals, item):
        tile_vals, rows_here, cols_here, alive = item
        row_select = (rows_here[:, None] == row_ids[None, :]).astype(jnp.bfloat16)
        picked = jnp.dot(row_select, flat_rows, preferred_element_type=jnp.float32).astype(
            jnp.bfloat16
        )
        picked = picked.reshape(group_size, tile_size, width)
        terms = jnp.einsum("tij,tif->tjf", tile_vals, picked, preferred_element_type=jnp.float32)
        col_select = (col_ids[:, None] == cols_here[None, :]).astype(jnp.float32) * alive[None, :]
        added = jnp.dot(
            col_select,
            terms.reshape(group_size, tile_size * width),
            precision=lax.Precision.HIGHEST,
        )
        return (totals + added, None)

    start = jnp.zeros((all_blocks, tile_size * width), jnp.float32)
    inputs = (
        tile_values.reshape(groups, group_size, tile_size, tile_size),
        tile_rows[0].reshape(groups, group_size),
        tile_cols[0].reshape(groups, group_size),
        live.reshape(groups, group_size),
    )
    adjoint = lax.scan(accumulate, start, inputs)[0]
    node_grad = lax.psum_scatter(
        adjoint.reshape(all_blocks * tile_size, width), "dom", scatter_dimension=0, tiled=True
    )
    return (node_grad, weight_grad)


def solution(mesh):
    return jax.shard_map(
        shards,
        mesh=mesh,
        in_specs=(
            P(("dom", "loop"), None),
            P(("dom", "loop"), None),
            P(("dom", "loop"), None),
            P(),
            P(("dom", "loop"), None, None),
            P(("dom", "loop"), None),
            P(("dom", "loop"), None),
            P(("dom", "loop")),
        ),
        out_specs=(P(("dom", "loop"), None), P()),
        check_vma=False,
    )
```

profile of v0, /device:TPU:1, one launch (start us, length us, event | category | flops | bytes accessed | tf_op | source)
XLA Modules:
  0.0 672.4 jit_solution(7241508006028594948)
XLA Ops:
  12.9 28.0 %copy.10 = bf16[640,128,128]{1,2,0:T(8,128)(2,1)} copy(bf16[640,128,128]{2,1,0:T(8,128)(2,1)} %param.14) | data formatting | bytes 41943040 | tf_op args[4]
  41.8 44.3 %all-gather.2.cloned.1.call-done = bf16[8192,256]{1,0:T(8,128)(2,1)} async-done(((bf16[1024,256]{1,0:T(8,128)(2,1)}), bf16[8192,256]{1,0:T(8,128)(2,1)}) %all-gather.2.cloned.1.call-update) | async-done | bytes 4194320 | tf_op jit(solution)/shard_map/all_gather | solution.py:22
  93.5 374.1 %while.11 = (s32[]{:T(128)}, f32[128,32768]{1,0:T(8,128)}, s32[10,64]{1,0:T(8,128)S(1)}, f32[10,64]{1,0:T(8,128)S(1)}, bf16[10,64,128,128]{2,3,1,0:T(8,128)(2,1)...) while((s32[]{:T(128)}, f32[128,32768]{1,0:T(8,128)}, ...), condition=%wide.region_1.2_spmd.clone, body=%wide.region_0.1_spmd.clone.sunk | while | flops 4037038080 | bytes 90180464 | solution.py:55
  101.0 8.0 %copy.17 = f32[8,8,128,256]{3,1,2,0:T(8,128)} copy(f32[8,8,128,256]{3,2,1,0:T(8,128)S(1)} %bitcast.44) | data formatting | bytes 16777216 | tf_op jit(solution)/shard_map/while
  108.9 19.9 %convolution_add_fusion.2 = f32[128,32768]{1,0:T(8,128)} fusion(f32[64,32768]{1,0:T(8,128)} %bitcast.43, f32[128,32768]{1,0:T(8,128)} %get-tuple-element.153, pred[]{:T(512)S(6)} %compare.3, f32[64]{0:T(128)S(1)} %fusion.41, s32[64]{0:T(128)S(1)} %get-tuple-element.142), kind=kOutput, calls=%fused_computation.2.clone.1 | convolution fusion | flops 3229630464 | bytes 41943552 | tf_op jit(solution)/shard_map/while/body/eval_jaxpr/dot_general | solution.py:41
  136.3 8.0 %copy.17 = f32[8,8,128,256]{3,1,2,0:T(8,128)} copy(f32[8,8,128,256]{3,2,1,0:T(8,128)S(1)} %bitcast.44) | data formatting | bytes 16777216 | tf_op jit(solution)/shard_map/while
  144.2 22.2 %convolution_add_fusion.2 = f32[128,32768]{1,0:T(8,128)} fusion(f32[64,32768]{1,0:T(8,128)} %bitcast.43, f32[128,32768]{1,0:T(8,128)} %get-tuple-element.153, pred[]{:T(512)S(6)} %compare.3, f32[64]{0:T(128)S(1)} %fusion.41, s32[64]{0:T(128)S(1)} %get-tuple-element.142), kind=kOutput, calls=%fused_computation.2.clone.1 | convolution fusion | flops 3229630464 | bytes 41943552 | tf_op jit(solution)/shard_map/while/body/eval_jaxpr/dot_general | solution.py:41
  173.9 8.0 %copy.17 = f32[8,8,128,256]{3,1,2,0:T(8,128)} copy(f32[8,8,128,256]{3,2,1,0:T(8,128)S(1)} %bitcast.44) | data formatting | bytes 16777216 | tf_op jit(solution)/shard_map/while
  181.9 22.2 %convolution_add_fusion.2 = f32[128,32768]{1,0:T(8,128)} fusion(f32[64,32768]{1,0:T(8,128)} %bitcast.43, f32[128,32768]{1,0:T(8,128)} %get-tuple-element.153, pred[]{:T(512)S(6)} %compare.3, f32[64]{0:T(128)S(1)} %fusion.41, s32[64]{0:T(128)S(1)} %get-tuple-element.142), kind=kOutput, calls=%fused_computation.2.clone.1 | convolution fusion | flops 3229630464 | bytes 41943552 | tf_op jit(solution)/shard_map/while/body/eval_jaxpr/dot_general | solution.py:41
  211.6 8.0 %copy.17 = f32[8,8,128,256]{3,1,2,0:T(8,128)} copy(f32[8,8,128,256]{3,2,1,0:T(8,128)S(1)} %bitcast.44) | data formatting | bytes 16777216 | tf_op jit(solution)/shard_map/while
  219.5 22.2 %convolution_add_fusion.2 = f32[128,32768]{1,0:T(8,128)} fusion(f32[64,32768]{1,0:T(8,128)} %bitcast.43, f32[128,32768]{1,0:T(8,128)} %get-tuple-element.153, pred[]{:T(512)S(6)} %compare.3, f32[64]{0:T(128)S(1)} %fusion.41, s32[64]{0:T(128)S(1)} %get-tuple-element.142), kind=kOutput, calls=%fused_computation.2.clone.1 | convolution fusion | flops 3229630464 | bytes 41943552 | tf_op jit(solution)/shard_map/while/body/eval_jaxpr/dot_general | solution.py:41
  249.2 8.0 %copy.17 = f32[8,8,128,256]{3,1,2,0:T(8,128)} copy(f32[8,8,128,256]{3,2,1,0:T(8,128)S(1)} %bitcast.44) | data formatting | bytes 16777216 | tf_op jit(solution)/shard_map/while
  257.2 22.2 %convolution_add_fusion.2 = f32[128,32768]{1,0:T(8,128)} fusion(f32[64,32768]{1,0:T(8,128)} %bitcast.43, f32[128,32768]{1,0:T(8,128)} %get-tuple-element.153, pred[]{:T(512)S(6)} %compare.3, f32[64]{0:T(128)S(1)} %fusion.41, s32[64]{0:T(128)S(1)} %get-tuple-element.142), kind=kOutput, calls=%fused_computation.2.clone.1 | convolution fusion | flops 3229630464 | bytes 41943552 | tf_op jit(solution)/shard_map/while/body/eval_jaxpr/dot_general | solution.py:41
  286.9 8.0 %copy.17 = f32[8,8,128,256]{3,1,2,0:T(8,128)} copy(f32[8,8,128,256]{3,2,1,0:T(8,128)S(1)} %bitcast.44) | data formatting | bytes 16777216 | tf_op jit(solution)/shard_map/while
  294.8 22.2 %convolution_add_fusion.2 = f32[128,32768]{1,0:T(8,128)} fusion(f32[64,32768]{1,0:T(8,128)} %bitcast.43, f32[128,32768]{1,0:T(8,128)} %get-tuple-element.153, pred[]{:T(512)S(6)} %compare.3, f32[64]{0:T(128)S(1)} %fusion.41, s32[64]{0:T(128)S(1)} %get-tuple-element.142), kind=kOutput, calls=%fused_computation.2.clone.1 | convolution fusion | flops 3229630464 | bytes 41943552 | tf_op jit(solution)/shard_map/while/body/eval_jaxpr/dot_general | solution.py:41
  324.5 8.0 %copy.17 = f32[8,8,128,256]{3,1,2,0:T(8,128)} copy(f32[8,8,128,256]{3,2,1,0:T(8,128)S(1)} %bitcast.44) | data formatting | bytes 16777216 | tf_op jit(solution)/shard_map/while
  332.5 22.2 %convolution_add_fusion.2 = f32[128,32768]{1,0:T(8,128)} fusion(f32[64,32768]{1,0:T(8,128)} %bitcast.43, f32[128,32768]{1,0:T(8,128)} %get-tuple-element.153, pred[]{:T(512)S(6)} %compare.3, f32[64]{0:T(128)S(1)} %fusion.41, s32[64]{0:T(128)S(1)} %get-tuple-element.142), kind=kOutput, calls=%fused_computation.2.clone.1 | convolution fusion | flops 3229630464 | bytes 41943552 | tf_op jit(solution)/shard_map/while/body/eval_jaxpr/dot_general | solution.py:41
  362.2 8.0 %copy.17 = f32[8,8,128,256]{3,1,2,0:T(8,128)} copy(f32[8,8,128,256]{3,2,1,0:T(8,128)S(1)} %bitcast.44) | data formatting | bytes 16777216 | tf_op jit(solution)/shard_map/while
  370.1 22.2 %convolution_add_fusion.2 = f32[128,32768]{1,0:T(8,128)} fusion(f32[64,32768]{1,0:T(8,128)} %bitcast.43, f32[128,32768]{1,0:T(8,128)} %get-tuple-element.153, pred[]{:T(512)S(6)} %compare.3, f32[64]{0:T(128)S(1)} %fusion.41, s32[64]{0:T(128)S(1)} %get-tuple-element.142), kind=kOutput, calls=%fused_computation.2.clone.1 | convolution fusion | flops 3229630464 | bytes 41943552 | tf_op jit(solution)/shard_map/while/body/eval_jaxpr/dot_general | solution.py:41
  399.8 8.0 %copy.17 = f32[8,8,128,256]{3,1,2,0:T(8,128)} copy(f32[8,8,128,256]{3,2,1,0:T(8,128)S(1)} %bitcast.44) | data formatting | bytes 16777216 | tf_op jit(solution)/shard_map/while
  407.8 22.2 %convolution_add_fusion.2 = f32[128,32768]{1,0:T(8,128)} fusion(f32[64,32768]{1,0:T(8,128)} %bitcast.43, f32[128,32768]{1,0:T(8,128)} %get-tuple-element.153, pred[]{:T(512)S(6)} %compare.3, f32[64]{0:T(128)S(1)} %fusion.41, s32[64]{0:T(128)S(1)} %get-tuple-element.142), kind=kOutput, calls=%fused_computation.2.clone.1 | convolution fusion | flops 3229630464 | bytes 41943552 | tf_op jit(solution)/shard_map/while/body/eval_jaxpr/dot_general | solution.py:41
  445.4 22.2 %convolution_add_fusion.2 = f32[128,32768]{1,0:T(8,128)} fusion(f32[64,32768]{1,0:T(8,128)} %bitcast.43, f32[128,32768]{1,0:T(8,128)} %get-tuple-element.153, pred[]{:T(512)S(6)} %compare.3, f32[64]{0:T(128)S(1)} %fusion.41, s32[64]{0:T(128)S(1)} %get-tuple-element.142), kind=kOutput, calls=%fused_computation.2.clone.1 | convolution fusion | flops 3229630464 | bytes 41943552 | tf_op jit(solution)/shard_map/while/body/eval_jaxpr/dot_general | solution.py:41
  467.7 18.0 %reshape.27 = f32[16384,256]{1,0:T(8,128)} reshape(f32[128,32768]{1,0:T(8,128)} %get-tuple-element.49) | data formatting | bytes 33554432 | tf_op jit(solution)/shard_map/reshape | solution.py:57
  487.5 177.4 %reduce-scatter.2.cloned.1.call-done = f32[1024,256]{1,0:T(8,128)} async-done(((f32[16384,256]{1,0:T(8,128)}), f32[1024,256]{1,0:T(8,128)}) %reduce-scatter.2.cloned.1.call-update) | async-done | bytes 1048592 | tf_op jit(solution)/shard_map/reduce_scatter | solution.py:56
  (76 shorter events, 96.7 us)
Async XLA Ops:
  8.0 2.5 copy-start
  8.0 78.1 %all-gather.2.cloned.1.call-start = ((), (), s32[]{:S(2)}) async-start(), calls=%async_computation.1 | async-start | bytes 4718592 | tf_op jit(solution)/shard_map/all_gather | solution.py:22
  10.5 475.2 %all-reduce.2.cloned.1.call-start = ((), (), s32[]{:S(2)}) async-start(), calls=%async_computation.3 | async-start | bytes 524288 | tf_op jit(solution)/shard_map/psum | solution.py:20
  12.9 652.1 %reduce-scatter.2.cloned.1.call-start = ((), (), s32[]{:S(2)}) async-start(), calls=%async_computation.2 | async-start | bytes 17825792 | tf_op jit(solution)/shard_map/reduce_scatter | solution.py:56
  12.9 28.0 %copy-start.2 = (s32[1,640]{1,0:T(1,128)S(1)}, s32[1,640]{1,0:T(1,128)}, u32[]{:S(2)}) copy-start(s32[1,640]{1,0:T(1,128)} %param.16) | copy-start | bytes 7684
  12.9 28.1 %copy-start.3 = (s32[1,640]{1,0:T(1,128)S(1)}, s32[1,640]{1,0:T(1,128)}, u32[]{:S(2)}) copy-start(s32[1,640]{1,0:T(1,128)} %param.15) | copy-start | bytes 7684
  485.6 179.3 %copy-start.1 = (bf16[1024,256]{1,0:T(8,128)(2,1)S(1)}, bf16[1024,256]{1,0:T(8,128)(2,1)}, u32[]{:S(2)}) copy-start(bf16[1024,256]{1,0:T(8,128)(2,1)} %param.12) | copy-start | bytes 1572868
Sparse Core Ops, SparseCore 0:
  11.8 74.3 all-gather.1
  485.8 179.1 reduce-scatter.1
Sparse Core Ops, SparseCore 1:
  16.3 169.7 all-reduce.1
where the time goes:
time: 676 us; the launch traced here: 672 us
  matrix products  288 us (43%)
  waiting for transfers between devices  222 us (33%)
  local copies, waits for them, and re-layouts  146 us (22%)
  between operations  16.2 us (2%)
    dot_general x10, matrix products, accumulate(): jnp.dot(col_select, terms.reshape(group_size, tile_size * width), precisi...  220 us
    reduce_scatter x1, waiting for transfers between devices, shards(): lax.psum_scatter(adjoint.reshape(all_blocks * tile_size, width), 'dom', s...  177 us
    while x20, local copies, waits for them, and re-layouts  90.5 us
    all_gather x1, waiting for transfers between devices, shards(): partition = lax.all_gather(projected, 'loop', axis=0, tiled=True)  44.3 us
    dot_general x10, matrix products, accumulate(): jnp.dot(row_select, flat_rows, preferred_element_type=jnp.float32)  34.8 us
    unnamed x10, local copies, waits for them, and re-layouts  29.9 us
    dot_general x10, matrix products, accumulate(): jnp.einsum('tij,tif->tjf', tile_vals, picked, preferred_element_type=jnp....  28.5 us
    reshape x1, local copies, waits for them, and re-layouts, shards(): adjoint.reshape(all_blocks * tile_size, width)  18 us
  transfers between devices with their start and end apart: 3, of which 2 were waited for; matrix products, arithmetic and copies ran while one was open for 64% of the time, Pallas kernels for 0%

commit v1 on v0

v1 whole, which is shorter than its diff:
```python
import functools
import math

import jax
import jax.numpy as jnp
from jax import lax
from jax.experimental import pallas as pl
from jax.experimental.pallas import tpu as pltpu
from jax.sharding import PartitionSpec as P

MESH = pl.DeviceIdType.MESH
VMEM = pl.BlockSpec(memory_space=pltpu.VMEM)
ANY = pl.BlockSpec(memory_space=pl.ANY)
F32 = jnp.float32
BF16 = jnp.bfloat16

ROWS = 1024
F = 256
TILE = 128
BLOCKS = 8
X = 4
LOOP = 8
Z = 4
CHUNKS = 4
GROUP = 64


def remote(src, dst, send, recv, where):
    return pltpu.make_async_remote_copy(
        src_ref=src, dst_ref=dst, send_sem=send, recv_sem=recv, device_id=where, device_id_type=MESH
    )


def greet(peers):
    barrier = pltpu.get_barrier_semaphore()
    for peer in peers:
        pl.semaphore_signal(barrier, inc=1, device_id=peer, device_id_type=MESH)
    return barrier, len(peers)


def gather_kernel(cot, pre, agg, w, out, wpart, masked, send, recv):
    me = lax.axis_index("loop")
    x, h = lax.rem(me, X), me // X
    right = {"loop": h * X + lax.rem(x + 1, X)}
    left = {"loop": h * X + lax.rem(x + X - 1, X)}
    across = {"loop": (1 - h) * X + x}
    barrier, arrivals = greet([right, left, across])

    size = ROWS // CHUNKS
    half = CHUNKS // 2

    def piece(high, step, c):
        return out.at[high * X + lax.rem(x + step, X), pl.ds(c * size, size)]

    def copy(kind, c, ref, where):
        return remote(ref, ref, send.at[kind, c], recv.at[kind, c], where)

    for c in range(CHUNKS):
        rows = pl.ds(c * size, size)
        live = jnp.where(pre[rows].astype(F32) > 0, cot[rows].astype(F32), 0.0).astype(BF16)
        masked[rows] = live
        out[me, rows] = lax.dot_general(
            live, w[...], (((1,), (1,)), ((), ())), preferred_element_type=F32
        ).astype(BF16)
    pl.semaphore_wait(barrier, arrivals)
    sent = []

    def go(kind, c, ref, where):
        op = copy(kind, c, ref, where)
        op.start()
        sent.append(op)

    def arrive(kind, c, ref):
        copy(kind, c, ref, right).wait_recv()

    back = [CHUNKS - 1 - c for c in range(CHUNKS)]
    for c in range(CHUNKS):
        go(0, c, piece(h, 0, c), right)
        go(1, back[c], piece(h, 0, back[c]), left)
        go(2, c, piece(h, 0, c), across)

    total = jnp.zeros((F, F), F32)
    for c in range(CHUNKS):
        rows = pl.ds(c * size, size)
        total += lax.dot_general(
            agg[rows], masked[rows], (((0,), (0,)), ((), ())), preferred_element_type=F32
        )
    wpart[...] = total

    for c in range(CHUNKS):
        b = back[c]
        arrive(0, c, piece(h, 3, c))
        if c < half:
            go(3, c, piece(h, 3, c), right)
        arrive(1, b, piece(h, 1, b))
        if b >= half:
            go(3, b, piece(h, 1, b), left)
        arrive(2, c, piece(1 - h, 0, c))
        go(4, c, piece(1 - h, 0, c), right)
        go(5, c, piece(1 - h, 0, c), left)
    for c in range(CHUNKS):
        arrive(4, c, piece(1 - h, 3, c))
        if c < half:
            go(6, c, piece(1 - h, 3, c), right)
        arrive(5, c, piece(1 - h, 1, c))
        if c >= half:
            go(6, c, piece(1 - h, 1, c), left)
    for c in range(CHUNKS):
        arrive(3, c, piece(h, 2, c))
    for c in range(CHUNKS):
        arrive(6, c, piece(1 - h, 2, c))
    for op in sent:
        op.wait_send()


def tiles_kernel(rows, cols, counts, tiles, part, own, sib, acc, narrow, sems):
    step = pl.program_id(0)
    core = lax.rem(lax.axis_index("dom"), 2)
    blocks = acc.shape[0] - 1
    half = blocks // 2

    @pl.when(step == 0)
    def _():
        def clear(i, _):
            acc[i] = jnp.zeros((TILE, F), F32)
            return 0

        lax.fori_loop(0, blocks, clear, 0)

    count = counts[0]

    def one(t):
        at = step * GROUP + t
        col = cols[at]
        pair = col // BLOCKS
        away = lax.rem(lax.rem(pair, 2) + core, 2)
        slot = away * half + pair // 2 * BLOCKS + lax.rem(col, BLOCKS)
        slot = jnp.where(at < count, slot, blocks)
        acc[slot] += lax.dot_general(
            tiles[t], part[rows[at]], (((0,), (0,)), ((), ())), preferred_element_type=F32
        )

    unroll = 8

    def body(i, _):
        for u in range(unroll):
            one(i * unroll + u)
        return 0

    lax.fori_loop(0, GROUP // unroll, body, 0)

    @pl.when(step == pl.num_programs(0) - 1)
    def _():
        mine = pltpu.make_async_copy(acc.at[pl.ds(0, half)], own, sems.at[0])
        mine.start()

        def shorten(i, _):
            narrow[i] = acc[half + i].astype(BF16)
            return 0

        lax.fori_loop(0, half, shorten, 0)
        other = pltpu.make_async_copy(narrow, sib, sems.at[1])
        other.start()
        mine.wait()
        other.wait()


def scatter_kernel(
    own_hbm, sib_hbm, wpart, node, wgrad,
    own, got, relay_in, final_in, outbox, ybox, yin, w_loop, w_z, w_pair, w_zall,
    load, sib_send, sib_recv, z_send, z_recv, y_send, y_recv, w_send, w_recv,
):
    dom, loop = lax.axis_index("dom"), lax.axis_index("loop")
    z, y, core = dom // 4, lax.rem(dom // 2, 2), lax.rem(dom, 2)

    def at(zz, yy, cc):
        return {"dom": zz * 4 + yy * 2 + cc}

    def zed(k):
        return lax.rem(z + k, Z)

    sibling = at(z, y, 1 - core)
    up, far, down = at(zed(1), y, core), at(zed(2), y, core), at(zed(3), y, core)
    over = at(z, 1 - y, core)
    diagonal = at(z, 1 - y, 1 - core)
    ring = [{"loop": lax.rem(loop + k, LOOP)} for k in range(1, LOOP)]
    barrier, arrivals = greet([sibling, up, far, down, over, diagonal] + ring)

    ys = (1 - y, y)
    order = [(2, 0), (1, 0), (3, 0), (2, 1), (1, 1), (3, 1), (0, 0), (0, 1)]
    loads = {}
    for k, i in order:
        op = pltpu.make_async_copy(own_hbm.at[zed(k), ys[i]], own.at[k, i], load.at[k, i])
        op.start()
        loads[k, i] = op
    pl.semaphore_wait(barrier, arrivals)
    sent = []

    def go(op):
        op.start()
        sent.append(op)

    def sib_copy(k, i):
        return remote(sib_hbm.at[zed(k), ys[i]], got.at[k, i], sib_send.at[k, i], sib_recv.at[k, i], sibling)

    for k, i in order:
        go(sib_copy(k, i))

    thin = F // LOOP // Z

    def w_copy(src, dst, s, r, where):
        return remote(src, dst, w_send.at[s], w_recv.at[r], where)

    def w_first():
        for k in range(1, LOOP):
            peer = lax.rem(loop + k, LOOP)
            go(w_copy(wpart.at[pl.ds(peer * 32, 32)], w_loop.at[k], k, k, ring[k - 1]))

    def w_second():
        for k in range(1, LOOP):
            w_copy(w_loop.at[k], w_loop.at[k], k, k, ring[0]).wait_recv()
        total = wpart[pl.ds(pl.multiple_of(loop * 32, 32), 32)]
        for k in range(1, LOOP):
            total += w_loop[k]
        w_loop[0] = total
        for k, where in ((1, up), (2, far), (3, down)):
            go(w_copy(w_loop.at[0, pl.ds(zed(k) * thin, thin)], w_z.at[k], 7 + k, 7 + k, where))

    def w_third():
        for k in range(1, Z):
            w_copy(w_z.at[k], w_z.at[k], 7 + k, 7 + k, up).wait_recv()
        total = w_loop[0, pl.ds(pl.multiple_of(z * thin, thin), thin)]
        for k in range(1, Z):
            total += w_z[k]
        w_pair[y * 2 + core] = total
        mine = w_pair.at[y * 2 + core]
        for k, where in ((0, sibling), (1, over), (2, diagonal)):
            go(w_copy(mine, mine, 11 + k, 11 + k, where))

    def w_fourth():
        spots = ((0, y * 2 + 1 - core), (1, (1 - y) * 2 + core), (2, (1 - y) * 2 + 1 - core))
        for k, spot in spots:
            w_copy(w_pair.at[spot], w_pair.at[spot], 11 + k, 11 + k, up).wait_recv()
        total = ((w_pair[0] + w_pair[1]) + (w_pair[2] + w_pair[3])) * (1.0 / math.sqrt(ROWS * 128))
        rows = pl.ds(pl.multiple_of(z * thin, thin), thin)
        w_zall[rows] = total
        for k, where in ((1, up), (2, far), (3, down)):
            go(w_copy(w_zall.at[rows], w_zall.at[rows], 13 + k, 13 + k, where))

    def w_fifth():
        for k in range(1, Z):
            rows = pl.ds(zed(Z - k) * thin, thin)
            w_copy(w_zall.at[rows], w_zall.at[rows], 13 + k, 13 + k, up).wait_recv()
        rows = pl.ds(pl.multiple_of(loop * 32, 32), 32)
        wgrad[rows] = w_zall[...]
        for k in range(1, LOOP):
            go(w_copy(w_zall, wgrad.at[rows], 16 + k, 16 + k, ring[k - 1]))

    def w_last():
        for k in range(1, LOOP):
            rows = pl.ds(lax.rem(loop + LOOP - k, LOOP) * 32, 32)
            w_copy(w_zall, wgrad.at[rows], 16 + k, 16 + k, ring[0]).wait_recv()

    w_first()

    size = ROWS // 2
    rows = [pl.ds(0, size), pl.ds(size, size)]
    ready = set()

    def chip(k, i, p):
        if (k, i) not in ready:
            ready.add((k, i))
            loads[k, i].wait()
            sib_copy(k, i).wait_recv()
        return own[k, i, rows[p]] + got[k, i, rows[p]].astype(F32)

    def z_copy(kind, i, p, src, dst, where):
        return remote(src, dst, z_send.at[kind, i, p], z_recv.at[kind, i, p], where)

    ways = (up, down)
    near = (1, 3)

    def start_far(i):
        for p in (0, 1):
            box = outbox.at[0, i, p]
            box[...] = chip(2, i, p).astype(BF16)
            go(z_copy(0, i, p, box, relay_in.at[i, p], ways[p]))

    def start_plain(i):
        for p in (0, 1):
            box = outbox.at[1, i, p]
            box[...] = chip(near[p], i, 1 - p).astype(BF16)
            go(z_copy(1, i, p, box, final_in.at[0, i, 1 - p], ways[p]))

    def start_relayed(i):
        for p in (0, 1):
            z_copy(0, i, p, relay_in.at[i, p], relay_in.at[i, p], up).wait_recv()
            box = outbox.at[2, i, p]
            box[...] = (chip(near[p], i, p) + relay_in[i, p].astype(F32)).astype(BF16)
            go(z_copy(2, i, p, box, final_in.at[1, i, p], ways[p]))

    def finish(i, p):
        z_copy(1, i, 1 - p, final_in.at[0, i, p], final_in.at[0, i, p], up).wait_recv()
        z_copy(2, i, p, final_in.at[1, i, p], final_in.at[1, i, p], up).wait_recv()
        return chip(0, i, p) + final_in[0, i, p].astype(F32) + final_in[1, i, p].astype(F32)

    start_far(0)
    start_plain(0)
    start_far(1)
    start_relayed(0)
    w_second()
    start_plain(1)
    w_third()
    for p in (0, 1):
        ybox[p] = finish(0, p).astype(BF16)
        go(remote(ybox.at[p], yin.at[p], y_send.at[p], y_recv.at[p], over))
    w_fourth()
    start_relayed(1)
    w_fifth()
    for p in (0, 1):
        total = finish(1, p)
        remote(ybox.at[p], yin.at[p], y_send.at[p], y_recv.at[p], over).wait_recv()
        node[rows[p]] = total + yin[p].astype(F32)
    w_last()
    for op in sent:
        op.wait_send()


def shards(cotangent, preact, aggregated, weight, tile_values, tile_rows, tile_cols, tile_counts):
    params = functools.partial(pltpu.CompilerParams, vmem_limit_bytes=56 * 1024 * 1024)
    dma = pltpu.SemaphoreType.DMA
    gathered, wpart = pl.pallas_call(
        gather_kernel,
        out_shape=(
            jax.ShapeDtypeStruct((LOOP, ROWS, F), BF16),
            jax.ShapeDtypeStruct((F, F), F32),
        ),
        in_specs=[VMEM] * 4,
        out_specs=(VMEM, VMEM),
        scratch_shapes=[pltpu.VMEM((ROWS, F), BF16), dma((7, CHUNKS)), dma((7, CHUNKS))],
        compiler_params=params(collective_id=0, has_side_effects=True),
        name="gather",
    )(cotangent, preact, aggregated, weight)

    slots = tile_rows.shape[1]
    blocks = LOOP * 2 * BLOCKS
    half = blocks // 2
    own, sib = pl.pallas_call(
        tiles_kernel,
        out_shape=(
            jax.ShapeDtypeStruct((half, TILE, F), F32),
            jax.ShapeDtypeStruct((half, TILE, F), BF16),
        ),
        grid_spec=pltpu.PrefetchScalarGridSpec(
            num_scalar_prefetch=3,
            grid=(slots // GROUP,),
            in_specs=[
                pl.BlockSpec((GROUP, TILE, TILE), lambda g, *_: (g, 0, 0)),
                pl.BlockSpec((LOOP * BLOCKS, TILE, F), lambda g, *_: (0, 0, 0)),
            ],
            out_specs=(ANY, ANY),
            scratch_shapes=[
                pltpu.VMEM((blocks + 1, TILE, F), F32),
                pltpu.VMEM((half, TILE, F), BF16),
                dma((2,)),
            ],
        ),
        compiler_params=params(),
        name="tiles",
    )(tile_rows[0], tile_cols[0], tile_counts, tile_values, gathered.reshape(LOOP * BLOCKS, TILE, F))

    part = (ROWS // 2, F)
    node, wgrad = pl.pallas_call(
        scatter_kernel,
        out_shape=(
            jax.ShapeDtypeStruct((ROWS, F), F32),
            jax.ShapeDtypeStruct((F, F), F32),
        ),
        in_specs=[ANY, ANY, VMEM],
        out_specs=(VMEM, VMEM),
        scratch_shapes=[
            pltpu.VMEM((Z, 2, ROWS, F), F32),
            pltpu.VMEM((Z, 2, ROWS, F), BF16),
            pltpu.VMEM((2, 2) + part, BF16),
            pltpu.VMEM((2, 2, 2) + part, BF16),
            pltpu.VMEM((3, 2, 2) + part, BF16),
            pltpu.VMEM((2,) + part, BF16),
            pltpu.VMEM((2,) + part, BF16),
            pltpu.VMEM((LOOP, F // LOOP, F), F32),
            pltpu.VMEM((Z, F // LOOP // Z, F), F32),
            pltpu.VMEM((4, F // LOOP // Z, F), F32),
            pltpu.VMEM((F // LOOP, F), F32),
            dma((Z, 2)), dma((Z, 2)), dma((Z, 2)),
            dma((3, 2, 2)), dma((3, 2, 2)),
            dma((2,)), dma((2,)),
            dma((24,)), dma((24,)),
        ],
        compiler_params=params(collective_id=1, has_side_effects=True),
        name="scatter",
    )(own.reshape(Z, 2, ROWS, F), sib.reshape(Z, 2, ROWS, F), wpart)
    return node, wgrad


def solution(mesh):
    split = P(("dom", "loop"))
    return jax.shard_map(
        shards,
        mesh=mesh,
        in_specs=(split, split, split, P(), split, split, split, split),
        out_specs=(split, P()),
        check_vma=False,
    )
```

time: 676 us -> 140 us (0.21)
  matrix products: 288 us -> 0 us
  waiting for transfers between devices: 222 us -> 0 us
  local copies, waits for them, and re-layouts: 146 us -> 3.93 us
  Pallas kernels: 0 us -> 132 us
  between operations: 16.2 us -> 1.3 us
    dot_general x32 -> x0, matrix products: 288 us -> none  [the longest x10 220 us: accumulate(): jnp.dot(col_select, terms.reshape(group_size, tile_size * width), precisi...]
    reduce_scatter x1 -> x0, waiting for transfers between devices: 177 us -> none  [shards(): lax.psum_scatter(adjoint.reshape(all_blocks * tile_size, width), 'dom', s...]
    pallas_call x0 -> x3, Pallas kernels: none -> 132 us  [the longest x1 51.6 us: shards(): pl.pallas_call(scatter_kernel, out_shape=(jax.ShapeDtypeStruct((ROWS, F),...]
    while x20 -> x0, local copies, waits for them, and re-layouts: 90.5 us -> none
    all_gather x1 -> x0, waiting for transfers between devices: 44.3 us -> none  [shards(): partition = lax.all_gather(projected, 'loop', axis=0, tiled=True)]
    unnamed x10 -> x2, local copies, waits for them, and re-layouts: 29.9 us -> 3.93 us
    reshape x2 -> x0, local copies, waits for them, and re-layouts: 25.4 us -> none  [the longest x1 18 us: shards(): adjoint.reshape(all_blocks * tile_size, width)]
  transfers between devices with their start and end apart: 3 -> 0, of which waited for: 2 -> 0; matrix products, arithmetic and copies ran while one was open for 64% -> 0% of each run, Pallas kernels for 0% -> 0%
where the time goes in v1:
time: 140 us
  Pallas kernels  132 us (94%)
  local copies, waits for them, and re-layouts  3.93 us (3%)
  other arithmetic  2.57 us (2%)
    pallas_call x1, Pallas kernels, shards(): pl.pallas_call(scatter_kernel, out_shape=(jax.ShapeDtypeStruct((ROWS, F),...  51.6 us
    pallas_call x1, Pallas kernels, shards(): pl.pallas_call(gather_kernel, out_shape=(jax.ShapeDtypeStruct((LOOP, ROWS...  44 us
    pallas_call x1, Pallas kernels, shards(): pl.pallas_call(tiles_kernel, out_shape=(jax.ShapeDtypeStruct((half, TILE,...  36.7 us
    unnamed x2, local copies, waits for them, and re-layouts  3.93 us

profile of v1, /device:TPU:1, one launch (start us, length us, event | category | flops | bytes accessed | tf_op | source)
XLA Modules:
  0.0 140.1 jit_solution(4422119445017200099)
XLA Ops:
  1.3 1.3 reduce.rows
  2.6 1.3 reduce.1.cols
  3.9 44.0 %gather.1 = (bf16[8,1024,256]{2,1,0:T(8,128)(2,1)}, f32[256,256]{1,0:T(8,128)}) custom-call(bf16[1024,256]{1,0:T(8,128)(2,1)} %cot.1, bf16[1024,256]{1,0:T(8,128)(2,1)} %pre.1, bf16[1024,256]{1,0:T(8,128)(2,1)} %agg.1, bf16[256,256]{1,0:T(8,128)(2,1)} %w.1), custom_call_target="tpu_custom_call" | custom-call | tf_op jit(solution)/shard_map/gather/pallas_call | solution.py:332
  47.8 36.7 %tiles.2 = (f32[64,128,256]{2,1,0:T(8,128)}, bf16[64,128,256]{2,1,0:T(8,128)(2,1)}) custom-call(s32[640]{0:T(1024)} %reduce.rows, s32[640]{0:T(1024)} %reduce.1.cols, s32[1]{0:T(128)S(6)} %copy.12.counts, bf16[640,128,128]{2,1,0:T(8,128)(2,1)} %tiles.3, bf16[64,128,256]{2,1,0:T(8,128)(2,1)} %bitcast.5), custom_call_target="tpu_custom_call" | custom-call | tf_op jit(solution)/shard_map/tiles/pallas_call | solution.py:348
  84.5 51.6 %scatter.1 = (f32[1024,256]{1,0:T(8,128)}, f32[256,256]{1,0:T(8,128)}) custom-call(f32[4,2,1024,256]{3,2,1,0:T(8,128)} %bitcast.3, bf16[4,2,1024,256]{3,2,1,0:T(8,128)(2,1)} %bitcast.4, f32[256,256]{1,0:T(8,128)} %get-tuple-element.9.wpart), custom_call_target="tpu_custom_call" | custom-call | tf_op jit(solution)/shard_map/scatter/pallas_call | solution.py:373
  136.1 2.3 %copy.13 = f32[1024,256]{1,0:T(8,128)} copy(f32[1024,256]{1,0:T(8,128)} %get-tuple-element.12) | data formatting | bytes 2097152
  138.4 1.7 %copy.14 = f32[256,256]{1,0:T(8,128)} copy(f32[256,256]{1,0:T(8,128)} %get-tuple-element.13) | data formatting | bytes 524288

commit v2 on v0

v2 whole, which is shorter than its diff:
```python
import functools
import math

import jax
import jax.numpy as jnp
from jax import lax
from jax.experimental import pallas as pl
from jax.experimental.pallas import tpu as pltpu
from jax.sharding import PartitionSpec as P

MESH = pl.DeviceIdType.MESH
VMEM = pl.BlockSpec(memory_space=pltpu.VMEM)
ANY = pl.BlockSpec(memory_space=pl.ANY)
F32 = jnp.float32
BF16 = jnp.bfloat16

ROWS = 1024
F = 256
TILE = 128
BLOCKS = 8
X = 4
LOOP = 8
Z = 4
HALF = F // 2
CHUNKS = 4
SLOTS = 640
STEPS = (SLOTS + 64) // 2
WIDE = 768
UNROLL = 32


def remote(src, dst, send, recv, where):
    return pltpu.make_async_remote_copy(
        src_ref=src, dst_ref=dst, send_sem=send, recv_sem=recv, device_id=where, device_id_type=MESH
    )


def greet(peers):
    barrier = pltpu.get_barrier_semaphore()
    for peer in peers:
        pl.semaphore_signal(barrier, inc=1, device_id=peer, device_id_type=MESH)
    return barrier, len(peers)


def plan_kernel(rows, cols, count, out):
    blocks = 128

    def iota(shape, axis):
        return lax.broadcasted_iota(jnp.int32, shape, axis)

    def pick(mask, value, axis):
        return jnp.sum(jnp.where(mask, value, 0.0), axis=axis, keepdims=True)

    live = iota((1, SLOTS), 1) < count[0]
    hit = (iota((blocks, SLOTS), 0) == cols[...]) & live
    hits = jnp.where(hit, 1.0, 0.0)
    number = jnp.sum(hits, axis=1, keepdims=True)
    steps = jnp.floor((number + 1.0) * 0.5)
    down, along = iota((blocks, blocks), 0), iota((blocks, blocks), 1)
    steps_row = pick(down == along, steps, 0)
    first = pick(along < down, steps_row, 1)
    first_row = pick(down < along, steps, 0)
    out[3:4, 0:blocks] = jnp.where(steps_row > 0, first_row + steps_row - 1.0, float(STEPS)).astype(jnp.int32)
    out[3:4, blocks:] = jnp.zeros((1, WIDE - blocks), jnp.int32)

    big = (SLOTS, SLOTS)
    earlier = jnp.where(iota(big, 0) < iota(big, 1), 1.0, 0.0).astype(BF16)
    rank = jnp.dot(hits.astype(BF16), earlier, preferred_element_type=F32)
    place = jnp.where(live, pick(hit, 2.0 * first + rank, 0), 1000.0)
    both = place * 64.0 + rows[...].astype(F32)
    both = pick(iota(big, 0) == iota(big, 1), both, 1)
    place = jnp.floor(both * (1.0 / 64.0))
    row = both - place * 64.0
    found = place.astype(jnp.int32) == iota((SLOTS, WIDE), 1)
    tile = pick(found, iota((SLOTS, WIDE), 0).astype(F32) - float(SLOTS), 0) + float(SLOTS)
    out[0:1] = tile.astype(jnp.int32)
    out[1:2] = pick(found, row, 0).astype(jnp.int32)
    opens = (first.astype(jnp.int32) == iota((blocks, WIDE), 1)) & (steps > 0)
    out[2:3] = (1.0 - jnp.max(jnp.where(opens, 1.0, 0.0), axis=0, keepdims=True)).astype(jnp.int32)


def layer_kernel(
    plan, cot, pre, agg, w, tiles_hbm, node, wgrad,
    tiles, part_a, part_b, masked, prefix, acc, own, sibbox, got, relay_in, final_in, outbox, ybox, yin,
    wpart, w_z, w_loop, w_pair, w_all,
    tile_sem, g_send, g_recv, s_send, s_recv, z_send, z_recv, y_send, y_recv, w_send, w_recv,
):
    dom, loop = lax.axis_index("dom"), lax.axis_index("loop")
    z, y, core = dom // 4, lax.rem(dom // 2, 2), lax.rem(dom, 2)
    x, high = lax.rem(loop, X), loop // X

    def at(zz, yy, cc):
        return {"dom": zz * 4 + yy * 2 + cc}

    def zed(k):
        return lax.rem(z + k, Z)

    sibling = at(z, y, 1 - core)
    up, far, down = at(zed(1), y, core), at(zed(2), y, core), at(zed(3), y, core)
    over = at(z, 1 - y, core)
    diagonal = at(z, 1 - y, 1 - core)
    right = {"loop": high * X + lax.rem(x + 1, X)}
    left = {"loop": high * X + lax.rem(x + X - 1, X)}
    across = {"loop": (1 - high) * X + x}
    ring = [{"loop": lax.rem(loop + k, LOOP)} for k in range(1, LOOP)]
    barrier, arrivals = greet([sibling, up, far, down, over, diagonal] + ring)

    load = pltpu.make_async_copy(tiles_hbm, tiles.at[pl.ds(0, SLOTS)], tile_sem)
    load.start()
    tiles[SLOTS] = jnp.zeros((TILE, TILE), BF16)
    prefix[STEPS] = jnp.zeros((TILE, HALF), BF16)
    sent = []

    def go(op):
        op.start()
        sent.append(op)

    part = (part_a, part_b)

    count = BLOCKS // CHUNKS

    def piece(f, hh, step, c):
        return part[f].at[pl.ds((hh * X + lax.rem(x + step, X)) * BLOCKS + c * count, count)]

    def g_copy(f, kind, c, ref, where):
        return remote(ref, ref, g_send.at[f, kind, c], g_recv.at[f, kind, c], where)

    def arrive(f, kind, c, ref):
        g_copy(f, kind, c, ref, right).wait_recv()

    back = [CHUNKS - 1 - c for c in range(CHUNKS)]

    def project(f):
        for c in range(2):
            rows = pl.ds(c * (ROWS // 2), ROWS // 2)
            if f == 0:
                masked[rows] = jnp.where(pre[rows].astype(F32) > 0, cot[rows].astype(F32), 0.0).astype(BF16)
            out = lax.dot_general(
                masked[rows], w[f * HALF:(f + 1) * HALF], (((1,), (1,)), ((), ())), preferred_element_type=F32
            )
            part[f][pl.ds(loop * BLOCKS + c * (BLOCKS // 2), BLOCKS // 2)] = out.astype(BF16).reshape(
                BLOCKS // 2, TILE, HALF
            )

    def gather_own(f):
        for c in range(CHUNKS):
            go(g_copy(f, 0, c, piece(f, high, 0, c), right))
            go(g_copy(f, 1, back[c], piece(f, high, 0, back[c]), left))
            go(g_copy(f, 2, c, piece(f, high, 0, c), across))

    def gather_on(f, chunks):
        for c in chunks:
            b = back[c]
            arrive(f, 0, c, piece(f, high, 3, c))
            if c < CHUNKS // 2:
                go(g_copy(f, 3, c, piece(f, high, 3, c), right))
            arrive(f, 1, b, piece(f, high, 1, b))
            if b >= CHUNKS // 2:
                go(g_copy(f, 3, b, piece(f, high, 1, b), left))
            arrive(f, 2, c, piece(f, 1 - high, 0, c))
            go(g_copy(f, 4, c, piece(f, 1 - high, 0, c), right))
            go(g_copy(f, 5, c, piece(f, 1 - high, 0, c), left))

    def gather_last(f):
        for c in range(CHUNKS):
            arrive(f, 4, c, piece(f, 1 - high, 3, c))
            if c < CHUNKS // 2:
                go(g_copy(f, 6, c, piece(f, 1 - high, 3, c), right))
            arrive(f, 5, c, piece(f, 1 - high, 1, c))
            if c >= CHUNKS // 2:
                go(g_copy(f, 6, c, piece(f, 1 - high, 1, c), left))

    def gather_end(f):
        for c in range(CHUNKS):
            arrive(f, 3, c, piece(f, high, 2, c))
        for c in range(CHUNKS):
            arrive(f, 6, c, piece(f, 1 - high, 2, c))

    thick, thin = F // Z, F // Z // LOOP

    def w_copy(src, dst, s, where):
        return remote(src, dst, w_send.at[s], w_recv.at[s], where)

    def own_rows(ref, index, size):
        return ref.at[pl.ds(pl.multiple_of(index * size, size), size)]

    def w_first():
        total = jnp.zeros((F, F), F32)
        for c in range(4):
            rows = pl.ds(c * (ROWS // 4), ROWS // 4)
            total += lax.dot_general(
                agg[rows], masked[rows], (((0,), (0,)), ((), ())), preferred_element_type=F32
            )
        wpart[...] = total
        for k, where in ((1, up), (2, far), (3, down)):
            go(w_copy(own_rows(wpart, zed(k), thick), w_z.at[k], k, where))

    def w_second():
        for k in range(1, Z):
            w_copy(w_z.at[k], w_z.at[k], k, up).wait_recv()
        total = own_rows(wpart, z, thick)[...]
        for k in range(1, Z):
            total += w_z[k]
        w_z[0] = total
        for k in range(1, LOOP):
            go(w_copy(own_rows(w_z.at[0], lax.rem(loop + k, LOOP), thin), w_loop.at[k], 3 + k, ring[k - 1]))

    def w_third():
        for k in range(1, LOOP):
            w_copy(w_loop.at[k], w_loop.at[k], 3 + k, up).wait_recv()
        total = own_rows(w_z.at[0], loop, thin)[...]
        for k in range(1, LOOP):
            total += w_loop[k]
        w_pair[y * 2 + core] = total
        mine = w_pair.at[y * 2 + core]
        for k, where in ((0, sibling), (1, over), (2, diagonal)):
            go(w_copy(mine, mine, 11 + k, where))

    def w_fourth():
        for k, spot in ((0, y * 2 + 1 - core), (1, (1 - y) * 2 + core), (2, (1 - y) * 2 + 1 - core)):
            w_copy(w_pair.at[spot], w_pair.at[spot], 11 + k, up).wait_recv()
        total = ((w_pair[0] + w_pair[1]) + (w_pair[2] + w_pair[3])) * (1.0 / math.sqrt(ROWS * 128))
        mine = own_rows(w_all, loop, thin)
        mine[...] = total
        for k in range(1, LOOP):
            go(w_copy(mine, mine, 13 + k, ring[k - 1]))

    def w_fifth():
        for k in range(1, LOOP):
            theirs = own_rows(w_all, lax.rem(loop + LOOP - k, LOOP), thin)
            w_copy(theirs, theirs, 13 + k, up).wait_recv()
        mine = own_rows(wgrad, z, thick)
        mine[...] = w_all[...]
        for k, where in ((1, up), (2, far), (3, down)):
            go(w_copy(w_all, mine, 20 + k, where))

    def w_last():
        for k in range(1, Z):
            w_copy(w_all, own_rows(wgrad, zed(Z - k), thick), 20 + k, up).wait_recv()

    def multiply(f, start, end):
        def one(s, total):
            pair = jnp.concatenate([tiles[plan[0, 2 * s]], tiles[plan[0, 2 * s + 1]]], axis=0)
            source = jnp.concatenate([part[f][plan[1, 2 * s]], part[f][plan[1, 2 * s + 1]]], axis=0)
            term = lax.dot_general(pair, source, (((0,), (0,)), ((), ())), preferred_element_type=F32)
            total = jnp.where(plan[2, s] != 0, total, 0.0) + term
            prefix[s] = total.astype(BF16)
            return total

        begin = jnp.zeros((TILE, HALF), F32) if start == 0 else acc[...]
        acc[...] = lax.fori_loop(start, end, one, begin, unroll=UNROLL)

    ys = (1 - y, y)
    order = [(2, 0), (1, 0), (3, 0), (2, 1), (1, 1), (3, 1), (0, 0), (0, 1)]

    def s_copy(f, k, i):
        return remote(sibbox.at[f, k, i], got.at[f, k, i], s_send.at[f, k, i], s_recv.at[f, k, i], sibling)

    def extract(f, box, k, i, cc):
        base = ((zed(k) * 2 + ys[i]) * 2 + cc) * BLOCKS

        def one(b, _):
            box[f, k, i, pl.ds(pl.multiple_of(b * TILE, TILE), TILE)] = prefix[plan[3, base + b]]
            return 0

        lax.fori_loop(0, BLOCKS, one, 0, unroll=BLOCKS)

    def split(f):
        for k, i in order:
            extract(f, sibbox, k, i, 1 - core)
            go(s_copy(f, k, i))
        for k, i in order:
            extract(f, own, k, i, core)

    size = ROWS // 2
    rows = [pl.ds(0, size), pl.ds(size, size)]
    ready = set()

    def chip(f, k, i, p):
        if (f, k, i) not in ready:
            ready.add((f, k, i))
            s_copy(f, k, i).wait_recv()
        return own[f, k, i, rows[p]].astype(F32) + got[f, k, i, rows[p]].astype(F32)

    def z_copy(f, kind, i, p, src, dst, where):
        return remote(src, dst, z_send.at[f, kind, i, p], z_recv.at[f, kind, i, p], where)

    ways = (up, down)
    near = (1, 3)

    def start_far(f, i):
        for p in (0, 1):
            box = outbox.at[f, 0, i, p]
            box[...] = chip(f, 2, i, p).astype(BF16)
            go(z_copy(f, 0, i, p, box, relay_in.at[f, i, p], ways[p]))

    def start_plain(f, i):
        for p in (0, 1):
            box = outbox.at[f, 1, i, p]
            box[...] = chip(f, near[p], i, 1 - p).astype(BF16)
            go(z_copy(f, 1, i, p, box, final_in.at[f, 0, i, 1 - p], ways[p]))

    def start_relayed(f, i):
        for p in (0, 1):
            z_copy(f, 0, i, p, relay_in.at[f, i, p], relay_in.at[f, i, p], up).wait_recv()
            box = outbox.at[f, 2, i, p]
            box[...] = (chip(f, near[p], i, p) + relay_in[f, i, p].astype(F32)).astype(BF16)
            go(z_copy(f, 2, i, p, box, final_in.at[f, 1, i, p], ways[p]))

    def finish(f, i, p):
        z_copy(f, 1, i, 1 - p, final_in.at[f, 0, i, p], final_in.at[f, 0, i, p], up).wait_recv()
        z_copy(f, 2, i, p, final_in.at[f, 1, i, p], final_in.at[f, 1, i, p], up).wait_recv()
        return chip(f, 0, i, p) + final_in[f, 0, i, p].astype(F32) + final_in[f, 1, i, p].astype(F32)

    def y_copy(f, p):
        return remote(ybox.at[f, p], yin.at[f, p], y_send.at[f, p], y_recv.at[f, p], over)

    def start_y(f):
        for p in (0, 1):
            ybox[f, p] = finish(f, 0, p).astype(BF16)
            go(y_copy(f, p))

    def end(f):
        for p in (0, 1):
            total = finish(f, 1, p)
            y_copy(f, p).wait_recv()
            node[rows[p], f * HALF:(f + 1) * HALF] = total + yin[f, p].astype(F32)

    cut = [0, 128, 256, STEPS]
    project(0)
    pl.semaphore_wait(barrier, arrivals)
    gather_own(0)
    project(1)
    w_first()
    gather_on(0, range(CHUNKS))
    w_second()
    gather_last(0)
    gather_own(1)
    w_third()
    gather_end(0)
    w_fourth()
    load.wait()
    multiply(0, cut[0], cut[1])
    w_fifth()
    multiply(0, cut[1], cut[2])
    gather_on(1, range(CHUNKS))
    multiply(0, cut[2], cut[3])
    split(0)
    gather_last(1)
    start_far(0, 0)
    start_plain(0, 0)
    start_far(0, 1)
    start_relayed(0, 0)
    start_plain(0, 1)
    gather_end(1)
    multiply(1, cut[0], cut[1])
    start_relayed(0, 1)
    multiply(1, cut[1], cut[2])
    start_y(0)
    multiply(1, cut[2], cut[3])
    split(1)
    start_far(1, 0)
    start_plain(1, 0)
    start_far(1, 1)
    end(0)
    start_relayed(1, 0)
    start_plain(1, 1)
    start_y(1)
    start_relayed(1, 1)
    end(1)
    w_last()
    for op in sent:
        op.wait_send()


def shards(cotangent, preact, aggregated, weight, tile_values, tile_rows, tile_cols, tile_counts):
    dma = pltpu.SemaphoreType.DMA
    SMEM = pl.BlockSpec(memory_space=pltpu.SMEM)
    plan = pl.pallas_call(
        plan_kernel,
        out_shape=jax.ShapeDtypeStruct((4, WIDE), jnp.int32),
        in_specs=[VMEM, VMEM, SMEM],
        out_specs=VMEM,
        name="plan",
    )(tile_rows, tile_cols, tile_counts)

    size = (ROWS // 2, HALF)
    thick, thin = F // Z, F // Z // LOOP
    node, wgrad = pl.pallas_call(
        layer_kernel,
        out_shape=(
            jax.ShapeDtypeStruct((ROWS, F), F32),
            jax.ShapeDtypeStruct((F, F), F32),
        ),
        in_specs=[SMEM] + [VMEM] * 4 + [ANY],
        out_specs=(VMEM, VMEM),
        scratch_shapes=[
            pltpu.VMEM((SLOTS + 1, TILE, TILE), BF16),
            pltpu.VMEM((LOOP * BLOCKS, TILE, HALF), BF16),
            pltpu.VMEM((LOOP * BLOCKS, TILE, HALF), BF16),
            pltpu.VMEM((ROWS, F), BF16),
            pltpu.VMEM((STEPS + 1, TILE, HALF), BF16),
            pltpu.VMEM((TILE, HALF), F32),
            pltpu.VMEM((2, Z, 2, ROWS, HALF), BF16),
            pltpu.VMEM((2, Z, 2, ROWS, HALF), BF16),
            pltpu.VMEM((2, Z, 2, ROWS, HALF), BF16),
            pltpu.VMEM((2, 2, 2) + size, BF16),
            pltpu.VMEM((2, 2, 2, 2) + size, BF16),
            pltpu.VMEM((2, 3, 2, 2) + size, BF16),
            pltpu.VMEM((2, 2) + size, BF16),
            pltpu.VMEM((2, 2) + size, BF16),
            pltpu.VMEM((F, F), F32),
            pltpu.VMEM((Z, thick, F), F32),
            pltpu.VMEM((LOOP, thin, F), F32),
            pltpu.VMEM((4, thin, F), F32),
            pltpu.VMEM((thick, F), F32),
            dma,
            dma((2, 7, CHUNKS)), dma((2, 7, CHUNKS)),
            dma((2, Z, 2)), dma((2, Z, 2)),
            dma((2, 3, 2, 2)), dma((2, 3, 2, 2)),
            dma((2, 2)), dma((2, 2)),
            dma((24,)), dma((24,)),
        ],
        compiler_params=pltpu.CompilerParams(
            vmem_limit_bytes=60 * 1024 * 1024, collective_id=0, has_side_effects=True
        ),
        name="layer",
    )(plan, cotangent, preact, aggregated, weight, tile_values)
    return node, wgrad


def solution(mesh):
    split = P(("dom", "loop"))
    return jax.shard_map(
        shards,
        mesh=mesh,
        in_specs=(split, split, split, P(), split, split, split, split),
        out_specs=(split, P()),
        check_vma=False,
    )
```

time: 676 us -> 103 us (0.15)
  matrix products: 288 us -> 0 us
  waiting for transfers between devices: 222 us -> 0 us
  local copies, waits for them, and re-layouts: 146 us -> 3.93 us
  Pallas kernels: 0 us -> 97.1 us
  between operations: 16.2 us -> 1.29 us
    dot_general x32 -> x0, matrix products: 288 us -> none  [the longest x10 220 us: accumulate(): jnp.dot(col_select, terms.reshape(group_size, tile_size * width), precisi...]
    reduce_scatter x1 -> x0, waiting for transfers between devices: 177 us -> none  [shards(): lax.psum_scatter(adjoint.reshape(all_blocks * tile_size, width), 'dom', s...]
    pallas_call x0 -> x2, Pallas kernels: none -> 97.1 us  [the longest x1 94.8 us: shards(): pl.pallas_call(layer_kernel, out_shape=(jax.ShapeDtypeStruct((ROWS, F), F...]
    while x20 -> x0, local copies, waits for them, and re-layouts: 90.5 us -> none
    all_gather x1 -> x0, waiting for transfers between devices: 44.3 us -> none  [shards(): partition = lax.all_gather(projected, 'loop', axis=0, tiled=True)]
    unnamed x10 -> x2, local copies, waits for them, and re-layouts: 29.9 us -> 3.93 us
    reshape x2 -> x0, local copies, waits for them, and re-layouts: 25.4 us -> none  [the longest x1 18 us: shards(): adjoint.reshape(all_blocks * tile_size, width)]
  transfers between devices with their start and end apart: 3 -> 0, of which waited for: 2 -> 0; matrix products, arithmetic and copies ran while one was open for 64% -> 0% of each run, Pallas kernels for 0% -> 0%
where the time goes in v2:
time: 103 us; the launch traced here: 102 us
  Pallas kernels  97.1 us (94%)
  local copies, waits for them, and re-layouts  3.93 us (4%)
  between operations  1.29 us (1%)
    pallas_call x1, Pallas kernels, shards(): pl.pallas_call(layer_kernel, out_shape=(jax.ShapeDtypeStruct((ROWS, F), F...  94.8 us
    unnamed x2, local copies, waits for them, and re-layouts  3.93 us
    pallas_call x1, Pallas kernels, shards(): pl.pallas_call(plan_kernel, out_shape=jax.ShapeDtypeStruct((4, WIDE), jnp...  2.28 us

profile of v2, /device:TPU:1, one launch (start us, length us, event | category | flops | bytes accessed | tf_op | source)
XLA Modules:
  0.0 102.3 jit_solution(3727441121127972516)
XLA Ops:
  1.3 2.3 %plan.1 = s32[4,768]{1,0:T(4,128)} custom-call(s32[1,640]{1,0:T(1,128)} %rows.1, s32[1,640]{1,0:T(1,128)} %cols.1, s32[1]{0:T(128)S(6)} %copy.12.count), custom_call_target="tpu_custom_call" | custom-call | tf_op jit(solution)/shard_map/plan/pallas_call | solution.py:379
  3.6 94.8 %layer.1 = (f32[1024,256]{1,0:T(8,128)}, f32[256,256]{1,0:T(8,128)}) custom-call(s32[4,768]{1,0:T(4,128)} %plan.1, bf16[1024,256]{1,0:T(8,128)(2,1)} %cot.1, bf16[1024,256]{1,0:T(8,128)(2,1)} %pre.1, bf16[1024,256]{1,0:T(8,128)(2,1)} %agg.1, bf16[256,256]{1,0:T(8,128)(2,1)} %w.1, bf16[640,128,128]{2,1,0:T(8,128)(2,1)} %tiles_hbm.1), custom_call_target="tpu_custom_call" | custom-call | tf_op jit(solution)/shard_map/layer/pallas_call | solution.py:389
  98.4 2.3 %copy.13 = f32[1024,256]{1,0:T(8,128)} copy(f32[1024,256]{1,0:T(8,128)} %get-tuple-element.4) | data formatting | bytes 2097152
  100.7 1.7 %copy.14 = f32[256,256]{1,0:T(8,128)} copy(f32[256,256]{1,0:T(8,128)} %get-tuple-element.5) | data formatting | bytes 524288

commit v3 on v2

--- a/solution.py
+++ b/solution.py
@@ -26,7 +26,8 @@
 SLOTS = 640
 STEPS = (SLOTS + 64) // 2
 WIDE = 768
-UNROLL = 32
+UNROLL = 88
+CROSS = ((1, 2), (1,))
 
 
 def remote(src, dst, send, recv, where):
@@ -136,33 +137,45 @@
             if f == 0:
                 masked[rows] = jnp.where(pre[rows].astype(F32) > 0, cot[rows].astype(F32), 0.0).astype(BF16)
             out = lax.dot_general(
-                masked[rows], w[f * HALF:(f + 1) * HALF], (((1,), (1,)), ((), ())), preferred_element_type=F32
-            )
-            part[f][pl.ds(loop * BLOCKS + c * (BLOCKS // 2), BLOCKS // 2)] = out.astype(BF16).reshape(
-                BLOCKS // 2, TILE, HALF
-            )
+                w[f * HALF:(f + 1) * HALF], masked[rows], (((1,), (1,)), ((), ())), preferred_element_type=F32
+            ).astype(BF16)
+            for b in range(BLOCKS // 2):
+                part[f][loop * BLOCKS + c * (BLOCKS // 2) + b] = out[:, b * TILE:(b + 1) * TILE]
 
     def gather_own(f):
-        for c in range(CHUNKS):
+        for c, b, a in zip(range(CHUNKS), back, crossing(f)):
             go(g_copy(f, 0, c, piece(f, high, 0, c), right))
-            go(g_copy(f, 1, back[c], piece(f, high, 0, back[c]), left))
-            go(g_copy(f, 2, c, piece(f, high, 0, c), across))
-
-    def gather_on(f, chunks):
-        for c in chunks:
-            b = back[c]
+            go(g_copy(f, 1, b, piece(f, high, 0, b), left))
+            go(g_copy(f, 2, a, piece(f, high, 0, a), across))
+
+    def crossing(f):
+        return sorted(range(CHUNKS), key=lambda c: c in CROSS[f])
+
+    def gather_on(f, turns):
+        for n in turns:
+            c, b, a = n, back[n], crossing(f)[n]
             arrive(f, 0, c, piece(f, high, 3, c))
             if c < CHUNKS // 2:
                 go(g_copy(f, 3, c, piece(f, high, 3, c), right))
+            if c in CROSS[f]:
+                go(g_copy(f, 4, c, piece(f, high, 3, c), across))
             arrive(f, 1, b, piece(f, high, 1, b))
             if b >= CHUNKS // 2:
                 go(g_copy(f, 3, b, piece(f, high, 1, b), left))
-            arrive(f, 2, c, piece(f, 1 - high, 0, c))
-            go(g_copy(f, 4, c, piece(f, 1 - high, 0, c), right))
-            go(g_copy(f, 5, c, piece(f, 1 - high, 0, c), left))
+            if b in CROSS[f]:
+                go(g_copy(f, 5, b, piece(f, high, 1, b), across))
+            arrive(f, 2, a, piece(f, 1 - high, 0, a))
+            if a not in CROSS[f]:
+                go(g_copy(f, 4, a, piece(f, 1 - high, 0, a), right))
+                go(g_copy(f, 5, a, piece(f, 1 - high, 0, a), left))
 
     def gather_last(f):
+        for c in CROSS[f]:
+            arrive(f, 3, c, piece(f, high, 2, c))
+            go(g_copy(f, 6, c, piece(f, high, 2, c), across))
         for c in range(CHUNKS):
+            if c in CROSS[f]:
+                continue
             arrive(f, 4, c, piece(f, 1 - high, 3, c))
             if c < CHUNKS // 2:
                 go(g_copy(f, 6, c, piece(f, 1 - high, 3, c), right))
@@ -172,8 +185,11 @@
 
     def gather_end(f):
         for c in range(CHUNKS):
-            arrive(f, 3, c, piece(f, high, 2, c))
-        for c in range(CHUNKS):
+            if c in CROSS[f]:
+                arrive(f, 4, c, piece(f, 1 - high, 3, c))
+                arrive(f, 5, c, piece(f, 1 - high, 1, c))
+            else:
+                arrive(f, 3, c, piece(f, high, 2, c))
             arrive(f, 6, c, piece(f, 1 - high, 2, c))
 
     thick, thin = F // Z, F // Z // LOOP
@@ -184,14 +200,14 @@
     def own_rows(ref, index, size):
         return ref.at[pl.ds(pl.multiple_of(index * size, size), size)]
 
+    def w_term(c):
+        rows = pl.ds(c * (ROWS // 4), ROWS // 4)
+        term = lax.dot_general(
+            agg[rows], masked[rows], (((0,), (0,)), ((), ())), preferred_element_type=F32
+        )
+        wpart[...] = term if c == 0 else wpart[...] + term
+
     def w_first():
-        total = jnp.zeros((F, F), F32)
-        for c in range(4):
-            rows = pl.ds(c * (ROWS // 4), ROWS // 4)
-            total += lax.dot_general(
-                agg[rows], masked[rows], (((0,), (0,)), ((), ())), preferred_element_type=F32
-            )
-        wpart[...] = total
         for k, where in ((1, up), (2, far), (3, down)):
             go(w_copy(own_rows(wpart, zed(k), thick), w_z.at[k], k, where))
 
@@ -241,13 +257,13 @@
     def multiply(f, start, end):
         def one(s, total):
             pair = jnp.concatenate([tiles[plan[0, 2 * s]], tiles[plan[0, 2 * s + 1]]], axis=0)
-            source = jnp.concatenate([part[f][plan[1, 2 * s]], part[f][plan[1, 2 * s + 1]]], axis=0)
-            term = lax.dot_general(pair, source, (((0,), (0,)), ((), ())), preferred_element_type=F32)
+            source = jnp.concatenate([part[f][plan[1, 2 * s]], part[f][plan[1, 2 * s + 1]]], axis=1)
+            term = jnp.dot(source, pair, preferred_element_type=F32)
             total = jnp.where(plan[2, s] != 0, total, 0.0) + term
             prefix[s] = total.astype(BF16)
             return total
 
-        begin = jnp.zeros((TILE, HALF), F32) if start == 0 else acc[...]
+        begin = jnp.zeros((HALF, TILE), F32) if start == 0 else acc[...]
         acc[...] = lax.fori_loop(start, end, one, begin, unroll=UNROLL)
 
     ys = (1 - y, y)
@@ -324,28 +340,30 @@
         for p in (0, 1):
             total = finish(f, 1, p)
             y_copy(f, p).wait_recv()
-            node[rows[p], f * HALF:(f + 1) * HALF] = total + yin[f, p].astype(F32)
-
-    cut = [0, 128, 256, STEPS]
+            total += yin[f, p].astype(F32)
+            for b in range(BLOCKS // 2):
+                place = pl.ds((p * (BLOCKS // 2) + b) * TILE, TILE)
+                node[place, f * HALF:(f + 1) * HALF] = total[b * TILE:(b + 1) * TILE].T
+
+    cut = [0, STEPS // 2, STEPS]
     project(0)
     pl.semaphore_wait(barrier, arrivals)
     gather_own(0)
     project(1)
+    for c in range(CHUNKS):
+        w_term(c)
+        gather_on(0, [c])
     w_first()
-    gather_on(0, range(CHUNKS))
-    w_second()
     gather_last(0)
     gather_own(1)
-    w_third()
     gather_end(0)
-    w_fourth()
     load.wait()
     multiply(0, cut[0], cut[1])
-    w_fifth()
+    w_second()
+    gather_on(1, range(CHUNKS))
     multiply(0, cut[1], cut[2])
-    gather_on(1, range(CHUNKS))
-    multiply(0, cut[2], cut[3])
     split(0)
+    w_third()
     gather_last(1)
     start_far(0, 0)
     start_plain(0, 0)
@@ -353,11 +371,12 @@
     start_relayed(0, 0)
     start_plain(0, 1)
     gather_end(1)
+    w_fourth()
     multiply(1, cut[0], cut[1])
     start_relayed(0, 1)
+    start_y(0)
+    w_fifth()
     multiply(1, cut[1], cut[2])
-    start_y(0)
-    multiply(1, cut[2], cut[3])
     split(1)
     start_far(1, 0)
     start_plain(1, 0)
@@ -371,6 +390,18 @@
     w_last()
     for op in sent:
         op.wait_send()
+
+
+def copy_kernel(node, wgrad, node_out, wgrad_out, sem):
+    rows = ROWS // 4
+    ops = [pltpu.make_async_copy(wgrad, wgrad_out, sem.at[4])]
+    for c in range(4):
+        part = pl.ds(c * rows, rows)
+        ops.append(pltpu.make_async_copy(node.at[part], node_out.at[part], sem.at[c]))
+    for op in ops:
+        op.start()
+    for op in ops:
+        op.wait()
 
 
 def shards(cotangent, preact, aggregated, weight, tile_values, tile_rows, tile_cols, tile_counts):
@@ -426,7 +457,17 @@
         ),
         name="layer",
     )(plan, cotangent, preact, aggregated, weight, tile_values)
-    return node, wgrad
+    return pl.pallas_call(
+        copy_kernel,
+        out_shape=(
+            jax.ShapeDtypeStruct((ROWS, F), F32),
+            jax.ShapeDtypeStruct((F, F), F32),
+        ),
+        in_specs=[ANY, ANY],
+        out_specs=(ANY, ANY),
+        scratch_shapes=[dma((5,))],
+        name="copies",
+    )(node, wgrad)
 
 
 def solution(mesh):

time: 103 us -> 128 us (1.24)
  Pallas kernels: 97.1 us -> 126 us
  local copies, waits for them, and re-layouts: 3.93 us -> 0 us
    pallas_call x0 -> x1, Pallas kernels: none -> 40.9 us  [shards(): pl.pallas_call(copy_kernel, out_shape=(jax.ShapeDtypeStruct((ROWS, F), F3...]
    pallas_call x1, Pallas kernels: 94.8 us -> 83.3 us  [shards(): pl.pallas_call(layer_kernel, out_shape=(jax.ShapeDtypeStruct((ROWS, F), F...]
    unnamed x2 -> x0, local copies, waits for them, and re-layouts: 3.93 us -> none
where the time goes in v3:
time: 128 us
  Pallas kernels  126 us (98%)
  between operations  1.29 us (1%)
    pallas_call x1, Pallas kernels, shards(): pl.pallas_call(layer_kernel, out_shape=(jax.ShapeDtypeStruct((ROWS, F), F...  83.3 us
    pallas_call x1, Pallas kernels, shards(): pl.pallas_call(copy_kernel, out_shape=(jax.ShapeDtypeStruct((ROWS, F), F3...  40.9 us

profile of v3, /device:TPU:1, one launch (start us, length us, event | category | flops | bytes accessed | tf_op | source)
XLA Modules:
  0.0 127.7 jit_solution(14581483031332939140)
XLA Ops:
  1.3 2.3 %plan.1 = s32[4,768]{1,0:T(4,128)} custom-call(s32[1,640]{1,0:T(1,128)} %rows.1, s32[1,640]{1,0:T(1,128)} %cols.1, s32[1]{0:T(128)S(6)} %copy.10.count), custom_call_target="tpu_custom_call" | custom-call | tf_op jit(solution)/shard_map/plan/pallas_call | solution.py:410
  3.6 83.3 %layer.1 = (f32[1024,256]{1,0:T(8,128)}, f32[256,256]{1,0:T(8,128)}) custom-call(s32[4,768]{1,0:T(4,128)} %plan.1, bf16[1024,256]{1,0:T(8,128)(2,1)} %cot.1, bf16[1024,256]{1,0:T(8,128)(2,1)} %pre.1, bf16[1024,256]{1,0:T(8,128)(2,1)} %agg.1, bf16[256,256]{1,0:T(8,128)(2,1)} %w.1, bf16[640,128,128]{2,1,0:T(8,128)(2,1)} %tiles_hbm.1), custom_call_target="tpu_custom_call" | custom-call | tf_op jit(solution)/shard_map/layer/pallas_call | solution.py:420
  86.9 40.9 %copies.1 = (f32[1024,256]{1,0:T(8,128)}, f32[256,256]{1,0:T(8,128)}) custom-call(f32[1024,256]{1,0:T(8,128)} %get-tuple-element.4.node, f32[256,256]{1,0:T(8,128)} %get-tuple-element.5.wgrad), custom_call_target="tpu_custom_call" | custom-call | tf_op jit(solution)/shard_map/copies/pallas_call | solution.py:460

commit v4 on v3

--- a/solution.py
+++ b/solution.py
@@ -82,9 +82,9 @@
 
 def layer_kernel(
     plan, cot, pre, agg, w, tiles_hbm, node, wgrad,
-    tiles, part_a, part_b, masked, prefix, acc, own, sibbox, got, relay_in, final_in, outbox, ybox, yin,
+    tiles, part_a, part_b, masked, prefix, acc, own, sibbox, got, relay_in, final_in, outbox, ybox, yin, xbox, xin,
     wpart, w_z, w_loop, w_pair, w_all,
-    tile_sem, g_send, g_recv, s_send, s_recv, z_send, z_recv, y_send, y_recv, w_send, w_recv,
+    tile_sem, g_send, g_recv, s_send, s_recv, z_send, z_recv, y_send, y_recv, x_send, x_recv, w_send, w_recv,
 ):
     dom, loop = lax.axis_index("dom"), lax.axis_index("loop")
     z, y, core = dom // 4, lax.rem(dom // 2, 2), lax.rem(dom, 2)
@@ -267,7 +267,7 @@
         acc[...] = lax.fori_loop(start, end, one, begin, unroll=UNROLL)
 
     ys = (1 - y, y)
-    order = [(2, 0), (1, 0), (3, 0), (2, 1), (1, 1), (3, 1), (0, 0), (0, 1)]
+    order = [(2, 0), (1, 0), (3, 0), (2, 1), (0, 0), (1, 1), (3, 1), (0, 1)]
 
     def s_copy(f, k, i):
         return remote(sibbox.at[f, k, i], got.at[f, k, i], s_send.at[f, k, i], s_recv.at[f, k, i], sibling)
@@ -285,48 +285,76 @@
         for k, i in order:
             extract(f, sibbox, k, i, 1 - core)
             go(s_copy(f, k, i))
+
+    taken = set()
+
+    def take(f, k, i):
+        if (f, k, i) not in taken:
+            taken.add((f, k, i))
+            extract(f, own, k, i, core)
+
+    def take_all(f):
         for k, i in order:
-            extract(f, own, k, i, core)
-
-    size = ROWS // 2
-    rows = [pl.ds(0, size), pl.ds(size, size)]
+            take(f, k, i)
+
+    size = ROWS // 4
     ready = set()
 
-    def chip(f, k, i, p):
+    def chip(f, k, i, p, q):
         if (f, k, i) not in ready:
             ready.add((f, k, i))
+            take(f, k, i)
             s_copy(f, k, i).wait_recv()
-        return own[f, k, i, rows[p]].astype(F32) + got[f, k, i, rows[p]].astype(F32)
-
-    def z_copy(f, kind, i, p, src, dst, where):
-        return remote(src, dst, z_send.at[f, kind, i, p], z_recv.at[f, kind, i, p], where)
+        rows = pl.ds((p * 2 + q) * size, size)
+        return own[f, k, i, rows].astype(F32) + got[f, k, i, rows].astype(F32)
+
+    def x_copy(f, k, p):
+        return remote(xbox.at[f, k, p], xin.at[f, k, p], x_send.at[f, k, p], x_recv.at[f, k, p], over)
+
+    def cross(f, k):
+        for p in (0, 1):
+            xbox[f, k, p] = chip(f, k, 0, p, 1).astype(BF16)
+            go(x_copy(f, k, p))
+
+    crossed = set()
+
+    def term(f, k, u, p):
+        if u < 2:
+            return chip(f, k, u, p, 0)
+        if (f, k, p) not in crossed:
+            crossed.add((f, k, p))
+            x_copy(f, k, p).wait_recv()
+        return chip(f, k, 1, p, 1) + xin[f, k, p].astype(F32)
+
+    def z_copy(f, kind, u, p, src, dst, where):
+        return remote(src, dst, z_send.at[f, kind, u, p], z_recv.at[f, kind, u, p], where)
 
     ways = (up, down)
     near = (1, 3)
 
-    def start_far(f, i):
-        for p in (0, 1):
-            box = outbox.at[f, 0, i, p]
-            box[...] = chip(f, 2, i, p).astype(BF16)
-            go(z_copy(f, 0, i, p, box, relay_in.at[f, i, p], ways[p]))
-
-    def start_plain(f, i):
-        for p in (0, 1):
-            box = outbox.at[f, 1, i, p]
-            box[...] = chip(f, near[p], i, 1 - p).astype(BF16)
-            go(z_copy(f, 1, i, p, box, final_in.at[f, 0, i, 1 - p], ways[p]))
-
-    def start_relayed(f, i):
-        for p in (0, 1):
-            z_copy(f, 0, i, p, relay_in.at[f, i, p], relay_in.at[f, i, p], up).wait_recv()
-            box = outbox.at[f, 2, i, p]
-            box[...] = (chip(f, near[p], i, p) + relay_in[f, i, p].astype(F32)).astype(BF16)
-            go(z_copy(f, 2, i, p, box, final_in.at[f, 1, i, p], ways[p]))
-
-    def finish(f, i, p):
-        z_copy(f, 1, i, 1 - p, final_in.at[f, 0, i, p], final_in.at[f, 0, i, p], up).wait_recv()
-        z_copy(f, 2, i, p, final_in.at[f, 1, i, p], final_in.at[f, 1, i, p], up).wait_recv()
-        return chip(f, 0, i, p) + final_in[f, 0, i, p].astype(F32) + final_in[f, 1, i, p].astype(F32)
+    def start_far(f, u):
+        for p in (0, 1):
+            box = outbox.at[f, 0, u, p]
+            box[...] = term(f, 2, u, p).astype(BF16)
+            go(z_copy(f, 0, u, p, box, relay_in.at[f, u, p], ways[p]))
+
+    def start_plain(f, u):
+        for p in (0, 1):
+            box = outbox.at[f, 1, u, p]
+            box[...] = term(f, near[p], u, 1 - p).astype(BF16)
+            go(z_copy(f, 1, u, p, box, final_in.at[f, 0, u, 1 - p], ways[p]))
+
+    def start_relayed(f, u):
+        for p in (0, 1):
+            z_copy(f, 0, u, p, relay_in.at[f, u, p], relay_in.at[f, u, p], up).wait_recv()
+            box = outbox.at[f, 2, u, p]
+            box[...] = (term(f, near[p], u, p) + relay_in[f, u, p].astype(F32)).astype(BF16)
+            go(z_copy(f, 2, u, p, box, final_in.at[f, 1, u, p], ways[p]))
+
+    def finish(f, u, p):
+        z_copy(f, 1, u, 1 - p, final_in.at[f, 0, u, p], final_in.at[f, 0, u, p], up).wait_recv()
+        z_copy(f, 2, u, p, final_in.at[f, 1, u, p], final_in.at[f, 1, u, p], up).wait_recv()
+        return term(f, 0, u, p) + final_in[f, 0, u, p].astype(F32) + final_in[f, 1, u, p].astype(F32)
 
     def y_copy(f, p):
         return remote(ybox.at[f, p], yin.at[f, p], y_send.at[f, p], y_recv.at[f, p], over)
@@ -336,14 +364,20 @@
             ybox[f, p] = finish(f, 0, p).astype(BF16)
             go(y_copy(f, p))
 
-    def end(f):
+    def write(f, p, q, total):
+        for b in range(2):
+            place = pl.ds(((p * 2 + q) * 2 + b) * TILE, TILE)
+            node[place, f * HALF:(f + 1) * HALF] = total[b * TILE:(b + 1) * TILE].T
+
+    def end_first(f):
         for p in (0, 1):
             total = finish(f, 1, p)
             y_copy(f, p).wait_recv()
-            total += yin[f, p].astype(F32)
-            for b in range(BLOCKS // 2):
-                place = pl.ds((p * (BLOCKS // 2) + b) * TILE, TILE)
-                node[place, f * HALF:(f + 1) * HALF] = total[b * TILE:(b + 1) * TILE].T
+            write(f, p, 0, total + yin[f, p].astype(F32))
+
+    def end_second(f):
+        for p in (0, 1):
+            write(f, p, 1, finish(f, 2, p))
 
     cut = [0, STEPS // 2, STEPS]
     project(0)
@@ -365,43 +399,53 @@
     split(0)
     w_third()
     gather_last(1)
+    cross(0, 2)
     start_far(0, 0)
     start_plain(0, 0)
+    cross(0, 1)
+    cross(0, 3)
     start_far(0, 1)
     start_relayed(0, 0)
     start_plain(0, 1)
+    cross(0, 0)
+    start_far(0, 2)
+    take_all(0)
     gather_end(1)
     w_fourth()
     multiply(1, cut[0], cut[1])
     start_relayed(0, 1)
+    start_plain(0, 2)
     start_y(0)
+    start_relayed(0, 2)
     w_fifth()
     multiply(1, cut[1], cut[2])
     split(1)
+    cross(1, 2)
     start_far(1, 0)
     start_plain(1, 0)
+    cross(1, 1)
+    cross(1, 3)
     start_far(1, 1)
-    end(0)
+    end_first(0)
     start_relayed(1, 0)
     start_plain(1, 1)
+    cross(1, 0)
+    start_far(1, 2)
+    start_relayed(1, 1)
+    start_plain(1, 2)
+    end_second(0)
     start_y(1)
-    start_relayed(1, 1)
-    end(1)
+    start_relayed(1, 2)
+    end_first(1)
+    end_second(1)
     w_last()
     for op in sent:
         op.wait_send()
 
 
-def copy_kernel(node, wgrad, node_out, wgrad_out, sem):
-    rows = ROWS // 4
-    ops = [pltpu.make_async_copy(wgrad, wgrad_out, sem.at[4])]
-    for c in range(4):
-        part = pl.ds(c * rows, rows)
-        ops.append(pltpu.make_async_copy(node.at[part], node_out.at[part], sem.at[c]))
-    for op in ops:
-        op.start()
-    for op in ops:
-        op.wait()
+def copy_kernel(node, wgrad, node_out, wgrad_out):
+    node_out[...] = node[...]
+    wgrad_out[...] = wgrad[...]
 
 
 def shards(cotangent, preact, aggregated, weight, tile_values, tile_rows, tile_cols, tile_counts):
@@ -415,7 +459,7 @@
         name="plan",
     )(tile_rows, tile_cols, tile_counts)
 
-    size = (ROWS // 2, HALF)
+    size = (ROWS // 4, HALF)
     thick, thin = F // Z, F // Z // LOOP
     node, wgrad = pl.pallas_call(
         layer_kernel,
@@ -435,11 +479,13 @@
             pltpu.VMEM((2, Z, 2, ROWS, HALF), BF16),
             pltpu.VMEM((2, Z, 2, ROWS, HALF), BF16),
             pltpu.VMEM((2, Z, 2, ROWS, HALF), BF16),
-            pltpu.VMEM((2, 2, 2) + size, BF16),
-            pltpu.VMEM((2, 2, 2, 2) + size, BF16),
-            pltpu.VMEM((2, 3, 2, 2) + size, BF16),
+            pltpu.VMEM((2, 3, 2) + size, BF16),
+            pltpu.VMEM((2, 2, 3, 2) + size, BF16),
+            pltpu.VMEM((2, 3, 3, 2) + size, BF16),
             pltpu.VMEM((2, 2) + size, BF16),
             pltpu.VMEM((2, 2) + size, BF16),
+            pltpu.VMEM((2, Z, 2) + size, BF16),
+            pltpu.VMEM((2, Z, 2) + size, BF16),
             pltpu.VMEM((F, F), F32),
             pltpu.VMEM((Z, thick, F), F32),
             pltpu.VMEM((LOOP, thin, F), F32),
@@ -448,8 +494,9 @@
             dma,
             dma((2, 7, CHUNKS)), dma((2, 7, CHUNKS)),
             dma((2, Z, 2)), dma((2, Z, 2)),
-            dma((2, 3, 2, 2)), dma((2, 3, 2, 2)),
+            dma((2, 3, 3, 2)), dma((2, 3, 3, 2)),
             dma((2, 2)), dma((2, 2)),
+            dma((2, Z, 2)), dma((2, Z, 2)),
             dma((24,)), dma((24,)),
         ],
         compiler_params=pltpu.CompilerParams(
@@ -463,9 +510,9 @@
             jax.ShapeDtypeStruct((ROWS, F), F32),
             jax.ShapeDtypeStruct((F, F), F32),
         ),
-        in_specs=[ANY, ANY],
-        out_specs=(ANY, ANY),
-        scratch_shapes=[dma((5,))],
+        grid=(4,),
+        in_specs=[pl.BlockSpec((ROWS // 4, F), lambda g: (g, 0)), pl.BlockSpec((F // 4, F), lambda g: (g, 0))],
+        out_specs=(pl.BlockSpec((ROWS // 4, F), lambda g: (g, 0)), pl.BlockSpec((F // 4, F), lambda g: (g, 0))),
         name="copies",
     )(node, wgrad)
 

time: 128 us -> 86.4 us (0.68)
  Pallas kernels: 126 us -> 84.9 us
    pallas_call x1, Pallas kernels: 40.9 us -> 3.41 us  [shards(): pl.pallas_call(copy_kernel, out_shape=(jax.ShapeDtypeStruct((ROWS, F), F3...]
    pallas_call x1, Pallas kernels: 83.3 us -> 79.2 us  [shards(): pl.pallas_call(layer_kernel, out_shape=(jax.ShapeDtypeStruct((ROWS, F), F...]
where the time goes in v4:
time: 86.4 us; the launch traced here: 86.1 us
  Pallas kernels  84.9 us (98%)
  between operations  1.29 us (1%)
    pallas_call x1, Pallas kernels, shards(): pl.pallas_call(layer_kernel, out_shape=(jax.ShapeDtypeStruct((ROWS, F), F...  79.2 us
    pallas_call x1, Pallas kernels, shards(): pl.pallas_call(copy_kernel, out_shape=(jax.ShapeDtypeStruct((ROWS, F), F3...  3.41 us
    pallas_call x1, Pallas kernels, shards(): pl.pallas_call(plan_kernel, out_shape=jax.ShapeDtypeStruct((4, WIDE), jnp...  2.28 us

profile of v4, /device:TPU:1, one launch (start us, length us, event | category | flops | bytes accessed | tf_op | source)
XLA Modules:
  0.0 86.1 jit_solution(921220856300216498)
XLA Ops:
  1.3 2.3 %plan.1 = s32[4,768]{1,0:T(4,128)} custom-call(s32[1,640]{1,0:T(1,128)} %rows.1, s32[1,640]{1,0:T(1,128)} %cols.1, s32[1]{0:T(128)S(6)} %copy.10.count), custom_call_target="tpu_custom_call" | custom-call | tf_op jit(solution)/shard_map/plan/pallas_call | solution.py:454
  3.6 79.2 %layer.1 = (f32[1024,256]{1,0:T(8,128)}, f32[256,256]{1,0:T(8,128)}) custom-call(s32[4,768]{1,0:T(4,128)} %plan.1, bf16[1024,256]{1,0:T(8,128)(2,1)} %cot.1, bf16[1024,256]{1,0:T(8,128)(2,1)} %pre.1, bf16[1024,256]{1,0:T(8,128)(2,1)} %agg.1, bf16[256,256]{1,0:T(8,128)(2,1)} %w.1, bf16[640,128,128]{2,1,0:T(8,128)(2,1)} %tiles_hbm.1), custom_call_target="tpu_custom_call" | custom-call | tf_op jit(solution)/shard_map/layer/pallas_call | solution.py:464
  82.7 3.4 %copies.1 = (f32[1024,256]{1,0:T(8,128)}, f32[256,256]{1,0:T(8,128)}) custom-call(f32[1024,256]{1,0:T(8,128)} %get-tuple-element.4.node, f32[256,256]{1,0:T(8,128)} %get-tuple-element.5.wgrad), custom_call_target="tpu_custom_call" | custom-call | tf_op jit(solution)/shard_map/copies/pallas_call | solution.py:507

commit v5 on v4

--- a/solution.py
+++ b/solution.py
@@ -81,10 +81,10 @@
 
 
 def layer_kernel(
-    plan, cot, pre, agg, w, tiles_hbm, node, wgrad,
-    tiles, part_a, part_b, masked, prefix, acc, own, sibbox, got, relay_in, final_in, outbox, ybox, yin, xbox, xin,
-    wpart, w_z, w_loop, w_pair, w_all,
-    tile_sem, g_send, g_recv, s_send, s_recv, z_send, z_recv, y_send, y_recv, x_send, x_recv, w_send, w_recv,
+    plan, cot_hbm, pre_hbm, agg_hbm, w_hbm, tiles_hbm, node, wgrad,
+    cot, pre, agg, w, tiles, part_a, part_b, masked, prefix, acc, own, sibbox, got, relay_in, final_in, outbox, ybox, yin, xbox, xin,
+    wpart, w_parts, w_z, w_loop, w_pair, w_all,
+    in_sem, tile_sem, g_send, g_recv, s_send, s_recv, z_send, z_recv, y_send, y_recv, x_send, x_recv, w_send, w_recv,
 ):
     dom, loop = lax.axis_index("dom"), lax.axis_index("loop")
     z, y, core = dom // 4, lax.rem(dom // 2, 2), lax.rem(dom, 2)
@@ -104,10 +104,15 @@
     left = {"loop": high * X + lax.rem(x + X - 1, X)}
     across = {"loop": (1 - high) * X + x}
     ring = [{"loop": lax.rem(loop + k, LOOP)} for k in range(1, LOOP)]
+    inputs = [
+        pltpu.make_async_copy(source, target, in_sem.at[n])
+        for n, (source, target) in enumerate(((pre_hbm, pre), (cot_hbm, cot), (w_hbm, w), (agg_hbm, agg)))
+    ]
+    for op in inputs:
+        op.start()
     barrier, arrivals = greet([sibling, up, far, down, over, diagonal] + ring)
 
     load = pltpu.make_async_copy(tiles_hbm, tiles.at[pl.ds(0, SLOTS)], tile_sem)
-    load.start()
     tiles[SLOTS] = jnp.zeros((TILE, TILE), BF16)
     prefix[STEPS] = jnp.zeros((TILE, HALF), BF16)
     sent = []
@@ -192,7 +197,7 @@
                 arrive(f, 3, c, piece(f, high, 2, c))
             arrive(f, 6, c, piece(f, 1 - high, 2, c))
 
-    thick, thin = F // Z, F // Z // LOOP
+    thin = F // Z // LOOP
 
     def w_copy(src, dst, s, where):
         return remote(src, dst, w_send.at[s], w_recv.at[s], where)
@@ -208,13 +213,16 @@
         wpart[...] = term if c == 0 else wpart[...] + term
 
     def w_first():
+        for k in range(Z):
+            for n in range(LOOP):
+                w_parts[k, n * thin:(n + 1) * thin] = wpart[(n * Z + k) * thin:(n * Z + k + 1) * thin]
         for k, where in ((1, up), (2, far), (3, down)):
-            go(w_copy(own_rows(wpart, zed(k), thick), w_z.at[k], k, where))
+            go(w_copy(w_parts.at[zed(k)], w_z.at[k], k, where))
 
     def w_second():
         for k in range(1, Z):
             w_copy(w_z.at[k], w_z.at[k], k, up).wait_recv()
-        total = own_rows(wpart, z, thick)[...]
+        total = w_parts[z]
         for k in range(1, Z):
             total += w_z[k]
         w_z[0] = total
@@ -236,23 +244,24 @@
         for k, spot in ((0, y * 2 + 1 - core), (1, (1 - y) * 2 + core), (2, (1 - y) * 2 + 1 - core)):
             w_copy(w_pair.at[spot], w_pair.at[spot], 11 + k, up).wait_recv()
         total = ((w_pair[0] + w_pair[1]) + (w_pair[2] + w_pair[3])) * (1.0 / math.sqrt(ROWS * 128))
-        mine = own_rows(w_all, loop, thin)
+        mine = own_rows(w_all, z, thin)
         mine[...] = total
+        for k, where in ((1, up), (2, far), (3, down)):
+            go(w_copy(mine, mine, 13 + k, where))
+
+    def w_fifth():
+        for k in range(1, Z):
+            theirs = own_rows(w_all, zed(Z - k), thin)
+            w_copy(theirs, theirs, 13 + k, up).wait_recv()
+        mine = own_rows(wgrad, loop, thin * Z)
+        mine[...] = w_all[...]
         for k in range(1, LOOP):
-            go(w_copy(mine, mine, 13 + k, ring[k - 1]))
-
-    def w_fifth():
+            go(w_copy(w_all, mine, 16 + k, ring[k - 1]))
+
+    def w_last():
         for k in range(1, LOOP):
-            theirs = own_rows(w_all, lax.rem(loop + LOOP - k, LOOP), thin)
-            w_copy(theirs, theirs, 13 + k, up).wait_recv()
-        mine = own_rows(wgrad, z, thick)
-        mine[...] = w_all[...]
-        for k, where in ((1, up), (2, far), (3, down)):
-            go(w_copy(w_all, mine, 20 + k, where))
-
-    def w_last():
-        for k in range(1, Z):
-            w_copy(w_all, own_rows(wgrad, zed(Z - k), thick), 20 + k, up).wait_recv()
+            theirs = own_rows(wgrad, lax.rem(loop + LOOP - k, LOOP), thin * Z)
+            w_copy(w_all, theirs, 16 + k, up).wait_recv()
 
     def multiply(f, start, end):
         def one(s, total):
@@ -379,7 +388,10 @@
         for p in (0, 1):
             write(f, p, 1, finish(f, 2, p))
 
-    cut = [0, STEPS // 2, STEPS]
+    cut = [0, 88, 176, 264, STEPS]
+    for op in inputs:
+        op.wait()
+    load.start()
     project(0)
     pl.semaphore_wait(barrier, arrivals)
     gather_own(0)
@@ -394,8 +406,11 @@
     load.wait()
     multiply(0, cut[0], cut[1])
     w_second()
-    gather_on(1, range(CHUNKS))
     multiply(0, cut[1], cut[2])
+    gather_on(1, [0, 1])
+    multiply(0, cut[2], cut[3])
+    gather_on(1, [2, 3])
+    multiply(0, cut[3], cut[4])
     split(0)
     w_third()
     gather_last(1)
@@ -415,10 +430,12 @@
     multiply(1, cut[0], cut[1])
     start_relayed(0, 1)
     start_plain(0, 2)
+    multiply(1, cut[1], cut[2])
+    start_relayed(0, 2)
+    multiply(1, cut[2], cut[3])
     start_y(0)
-    start_relayed(0, 2)
     w_fifth()
-    multiply(1, cut[1], cut[2])
+    multiply(1, cut[3], cut[4])
     split(1)
     cross(1, 2)
     start_far(1, 0)
@@ -467,9 +484,13 @@
             jax.ShapeDtypeStruct((ROWS, F), F32),
             jax.ShapeDtypeStruct((F, F), F32),
         ),
-        in_specs=[SMEM] + [VMEM] * 4 + [ANY],
+        in_specs=[SMEM] + [ANY] * 5,
         out_specs=(VMEM, VMEM),
         scratch_shapes=[
+            pltpu.VMEM((ROWS, F), BF16),
+            pltpu.VMEM((ROWS, F), BF16),
+            pltpu.VMEM((ROWS, F), BF16),
+            pltpu.VMEM((F, F), BF16),
             pltpu.VMEM((SLOTS + 1, TILE, TILE), BF16),
             pltpu.VMEM((LOOP * BLOCKS, TILE, HALF), BF16),
             pltpu.VMEM((LOOP * BLOCKS, TILE, HALF), BF16),
@@ -488,10 +509,11 @@
             pltpu.VMEM((2, Z, 2) + size, BF16),
             pltpu.VMEM((F, F), F32),
             pltpu.VMEM((Z, thick, F), F32),
+            pltpu.VMEM((Z, thick, F), F32),
             pltpu.VMEM((LOOP, thin, F), F32),
             pltpu.VMEM((4, thin, F), F32),
-            pltpu.VMEM((thick, F), F32),
-            dma,
+            pltpu.VMEM((Z * thin, F), F32),
+            dma((4,)), dma,
             dma((2, 7, CHUNKS)), dma((2, 7, CHUNKS)),
             dma((2, Z, 2)), dma((2, Z, 2)),
             dma((2, 3, 3, 2)), dma((2, 3, 3, 2)),
@@ -510,9 +532,8 @@
             jax.ShapeDtypeStruct((ROWS, F), F32),
             jax.ShapeDtypeStruct((F, F), F32),
         ),
-        grid=(4,),
-        in_specs=[pl.BlockSpec((ROWS // 4, F), lambda g: (g, 0)), pl.BlockSpec((F // 4, F), lambda g: (g, 0))],
-        out_specs=(pl.BlockSpec((ROWS // 4, F), lambda g: (g, 0)), pl.BlockSpec((F // 4, F), lambda g: (g, 0))),
+        in_specs=[VMEM, VMEM],
+        out_specs=(VMEM, VMEM),
         name="copies",
     )(node, wgrad)
 

time: 86.4 us -> 81 us (0.937)
  Pallas kernels: 84.9 us -> 79.5 us
    pallas_call x1, Pallas kernels: 79.2 us -> 74.8 us  [shards(): pl.pallas_call(layer_kernel, out_shape=(jax.ShapeDtypeStruct((ROWS, F), F...]
    pallas_call x1, Pallas kernels: 3.41 us -> 2.38 us  [shards(): pl.pallas_call(copy_kernel, out_shape=(jax.ShapeDtypeStruct((ROWS, F), F3...]
where the time goes in v5:
time: 81 us; the launch traced here: 80.8 us
  Pallas kernels  79.5 us (98%)
  between operations  1.29 us (2%)
    pallas_call x1, Pallas kernels, shards(): pl.pallas_call(layer_kernel, out_shape=(jax.ShapeDtypeStruct((ROWS, F), F...  74.8 us
    pallas_call x1, Pallas kernels, shards(): pl.pallas_call(copy_kernel, out_shape=(jax.ShapeDtypeStruct((ROWS, F), F3...  2.38 us
    pallas_call x1, Pallas kernels, shards(): pl.pallas_call(plan_kernel, out_shape=jax.ShapeDtypeStruct((4, WIDE), jnp...  2.28 us

profile of v5, /device:TPU:1, one launch (start us, length us, event | category | flops | bytes accessed | tf_op | source)
XLA Modules:
  0.0 80.8 jit_solution(6773538945259874183)
XLA Ops:
  1.3 2.3 %plan.1 = s32[4,768]{1,0:T(4,128)} custom-call(s32[1,640]{1,0:T(1,128)} %rows.1, s32[1,640]{1,0:T(1,128)} %cols.1, s32[1]{0:T(128)S(6)} %copy.10.count), custom_call_target="tpu_custom_call" | custom-call | tf_op jit(solution)/shard_map/plan/pallas_call | solution.py:471
  3.6 74.8 %layer.1 = (f32[1024,256]{1,0:T(8,128)}, f32[256,256]{1,0:T(8,128)}) custom-call(s32[4,768]{1,0:T(4,128)} %plan.1, bf16[1024,256]{1,0:T(8,128)(2,1)} %cot_hbm.1, bf16[1024,256]{1,0:T(8,128)(2,1)} %pre_hbm.1, bf16[1024,256]{1,0:T(8,128)(2,1)} %agg_hbm.1, bf16[256,256]{1,0:T(8,128)(2,1)} %w_hbm.1, bf16[640,128,128]{2,1,0:T(8,128)(2,1)} %tiles_hbm.1), custom_call_target="tpu_custom_call" | custom-call | tf_op jit(solution)/shard_map/layer/pallas_call | solution.py:481
  78.4 2.4 %copies.1 = (f32[1024,256]{1,0:T(8,128)}, f32[256,256]{1,0:T(8,128)}) custom-call(f32[1024,256]{1,0:T(8,128)} %get-tuple-element.4.node, f32[256,256]{1,0:T(8,128)} %get-tuple-element.5.wgrad), custom_call_target="tpu_custom_call" | custom-call | tf_op jit(solution)/shard_map/copies/pallas_call | solution.py:529
